TPU v7x, 256 devices: a whole 4x4x8 slice. The times are simulated.
256 devices in a mesh: tile: 32 (over x, y, core), lev: 8 (over z).
Axes of the slice: x: 4, y: 4, z: 8, core: 2. Of those that a mesh axis runs over, the one named last changes fastest.
Arguments:
- field: float32 [32, 40, 256, 256], P('tile', 'lev'), may hold values from -6 to 6
- kappa_x: float32 [32, 256, 256], P('tile'), may hold values from 0.04 to 0.12
- kappa_y: float32 [32, 256, 256], P('tile'), may hold values from 0.04 to 0.12
- sea_mask: int32 [32, 256, 256], P('tile'), may hold values 0 or 1
- tile_links: int32 [32, 4], P('tile'), may hold values from -1 to 127, as said below
- vertical: bfloat16 [40, 40], replicated, may hold values from -1 to 1
Outputs:
- correlated: float32 [32, 40, 256, 256], P('tile', 'lev')
Inputs may be any that keep to these rules, and one draw needn't show every extreme that they name: `tile_links`: tile n lies in column n of a single row of G = 32 columns that wraps east-west. West and east links go to the same row of the previous and next column (to its east and west face), no tile has a south link, and the north link of every tile is always present and goes to the top-row tile of column (G - c) % G, to its north face. A link of tile n to tile m is present exactly when the matching link of m to n is.
All inputs are finite; a program needn't handle non-finite values. No bound on the sum of `sea_mask` on one device may be relied on, other than what follows from the above.
Results may differ from a plain program's by a relative error of at most 0.0029.
Values may be sent and summed in bfloat16 or wider, within the bound.
No kernel may reach another device: no remote copies, remote signals or barrier semaphores. Data moves between devices by JAX's collectives and lax.ppermute only.
A program may use at most 128 MiB of HBM per device.

v0:
```python
import jax
import jax.numpy as jnp
from jax import lax
from jax.sharding import PartitionSpec as P

STEPS = 10


def faces_of(values):
    return jnp.stack(
        [values[..., :, 0], values[..., :, -1], values[..., 0, :], values[..., -1, :]], axis=1
    )


def place(fetched, linked, reverse):
    trailing = (1,) * (fetched.ndim - 2)
    fetched = jnp.where(reverse.reshape(reverse.shape + trailing), jnp.flip(fetched, -1), fetched)
    return jnp.where(linked.reshape(linked.shape + trailing), fetched, jnp.zeros_like(fetched))


def neighbours(values, rim_cells):
    west_cells = jnp.concatenate([rim_cells[:, 0, ..., None], values[..., :, :-1]], axis=-1)
    east_cells = jnp.concatenate([values[..., :, 1:], rim_cells[:, 1, ..., None]], axis=-1)
    south_cells = jnp.concatenate([rim_cells[:, 2, ..., None, :], values[..., :-1, :]], axis=-2)
    north_cells = jnp.concatenate([values[..., 1:, :], rim_cells[:, 3, ..., None, :]], axis=-2)
    return (west_cells, east_cells, south_cells, north_cells)


def pair_weights(statics, rim_cells):
    west_cells, east_cells, south_cells, north_cells = neighbours(statics, rim_cells)
    sea_cells = statics[:, 0]
    to_west = 0.5 * (statics[:, 1] + west_cells[:, 1]) * sea_cells * west_cells[:, 0]
    to_east = 0.5 * (statics[:, 1] + east_cells[:, 1]) * sea_cells * east_cells[:, 0]
    to_south = 0.5 * (statics[:, 2] + south_cells[:, 2]) * sea_cells * south_cells[:, 0]
    to_north = 0.5 * (statics[:, 2] + north_cells[:, 2]) * sea_cells * north_cells[:, 0]
    return (to_west, to_east, to_south, to_north)


def diffuse(current, rim_cells, weights):
    west_cells, east_cells, south_cells, north_cells = neighbours(current, rim_cells)
    to_west, to_east, to_south, to_north = weights
    return current + (
        to_west * (west_cells - current)
        + to_east * (east_cells - current)
        + to_south * (south_cells - current)
        + to_north * (north_cells - current)
    )


def shards(field, kappa_x, kappa_y, sea_mask, tile_links, vertical):
    per_dev = field.shape[0]
    lev_dev = field.shape[1]
    tile_edge = field.shape[-1]
    sea_cells = sea_mask.astype(jnp.float32)
    side_ids = jnp.arange(4, dtype=jnp.int32)[None, :]
    linked = tile_links >= 0
    reverse = linked & (tile_links % 4 == side_ids)
    position = jnp.where(linked, tile_links, 0)

    def rims_of(values):
        tile_faces = faces_of(values)
        flat_shape = (-1,) + tile_faces.shape[2:]
        face_pool = lax.all_gather(tile_faces, "tile", axis=0, tiled=True).reshape(flat_shape)
        return place(jnp.take(face_pool, position, axis=0), linked, reverse)

    statics = jnp.stack([sea_cells, kappa_x, kappa_y], axis=1)
    weights = tuple((weight[:, None] for weight in pair_weights(statics, rims_of(statics))))
    current = field * sea_cells[:, None]

    def one_step(step_number, values):
        return diffuse(values, rims_of(values), weights)

    current = lax.fori_loop(0, STEPS, one_step, current)
    smooth = current.astype(jnp.bfloat16).reshape(per_dev, lev_dev, tile_edge * tile_edge)
    lev_index = lax.axis_index("lev")
    own_rows = lax.dynamic_slice_in_dim(vertical, lev_index * lev_dev, lev_dev, 0)
    result = jnp.einsum(
        "kr,frn->fkn",
        own_rows,
        lax.all_gather(smooth, "lev", axis=1, tiled=True),
        preferred_element_type=jnp.float32,
    )
    return result.reshape(field.shape)


def solution(mesh):
    placed = (
        P("tile", "lev", None, None),
        P("tile", None, None),
        P("tile", None, None),
        P("tile", None, None),
        P("tile", None),
        P(),
    )
    return jax.shard_map(
        shards, mesh=mesh, in_specs=placed, out_specs=P("tile", "lev", None, None), check_vma=False
    )
```

profile of v0, /device:TPU:15, one launch (start us, length us, event | category | flops | bytes accessed | tf_op | source)
XLA Modules:
  0.0 660.3 jit_solution(16728557823721878549)
XLA Ops:
  13.3 4.6 slice_reduce_fusion.1
  18.7 2.1 fusion.45
  21.6 24.0 %all_gather.9 = f32[32,4,3,256]{3,1,2,0:T(4,128)S(1)} all-gather(f32[1,4,3,256]{3,1,2,0:T(4,128)S(1)} %pad_maximum_fusion.6), channel_id=1, replica_groups=mesh['tile'=32,'lev'=8] {'tile'}, dimensions={0}, use_global_device_ids=true | all-gather | bytes 405504 | tf_op jit(solution)/shard_map/all_gather | solution.py:63
  53.0 5.0 fusion.33
  60.8 463.3 %while.10 = (s32[]{:T(128)}, f32[1,5,256,256]{3,0,2,1:T(1,128)S(1)}, f32[1,1,256,256]{3,2,1,0:T(8,128)S(1)}, pred[1,4]{1,0:T(4,128)(4,1)S(1)}, pred[1,4]{1,0:T(4...) while((s32[]{:T(128)}, ...), condition=%wide.region_1.2_spmd, body=%wide.region_0.1_spmd.sunk | while | flops 5279782 | bytes 24297672 | solution.py:73
  61.1 3.3 copy.146
  64.4 23.7 %all_gather.12 = f32[32,4,5,256]{3,1,2,0:T(4,128)S(1)} all-gather(f32[1,4,5,256]{3,1,2,0:T(4,128)S(1)} %pad_maximum_fusion.8), channel_id=1, replica_groups=mesh['tile'=32,'lev'=8] {'tile'}, dimensions={0}, use_global_device_ids=true | all-gather | bytes 675840 | tf_op jit(solution)/shard_map/while/body/eval_jaxpr/all_gather | solution.py:63
  91.4 3.6 fusion.52
  95.0 12.6 %fusion.53 = f32[1,5,256,256]{3,0,2,1:T(1,128)S(1)} fusion(f32[1,5,256,256]{3,0,2,1:T(1,128)S(1)} %get-tuple-element.217, f32[1,5,1,256]{3,0,2,1:T(1,128)S(1)} %get-tuple-element.198, f32[1,5,255,256]{3,0,2,1:T(1,128)S(1)} %get-tuple-element.199, f32[1,5,255,256]{3,0,2,1:T(1,128)S(1)} %get-tuple-element.200, ...), kind=kLoop, calls=%fused_computation.13.clone.1 | loop fusion | flops 5242880 | bytes 8912896 | tf_op jit(solution)/shard_map/while/body/eval_jaxpr/add | solution.py:42
  107.7 3.3 copy.146
  111.0 23.0 %all_gather.12 = f32[32,4,5,256]{3,1,2,0:T(4,128)S(1)} all-gather(f32[1,4,5,256]{3,1,2,0:T(4,128)S(1)} %pad_maximum_fusion.8), channel_id=1, replica_groups=mesh['tile'=32,'lev'=8] {'tile'}, dimensions={0}, use_global_device_ids=true | all-gather | bytes 675840 | tf_op jit(solution)/shard_map/while/body/eval_jaxpr/all_gather | solution.py:63
  137.3 3.6 fusion.52
  140.9 12.6 %fusion.53 = f32[1,5,256,256]{3,0,2,1:T(1,128)S(1)} fusion(f32[1,5,256,256]{3,0,2,1:T(1,128)S(1)} %get-tuple-element.217, f32[1,5,1,256]{3,0,2,1:T(1,128)S(1)} %get-tuple-element.198, f32[1,5,255,256]{3,0,2,1:T(1,128)S(1)} %get-tuple-element.199, f32[1,5,255,256]{3,0,2,1:T(1,128)S(1)} %get-tuple-element.200, ...), kind=kLoop, calls=%fused_computation.13.clone.1 | loop fusion | flops 5242880 | bytes 8912896 | tf_op jit(solution)/shard_map/while/body/eval_jaxpr/add | solution.py:42
  153.6 3.3 copy.146
  157.0 23.8 %all_gather.12 = f32[32,4,5,256]{3,1,2,0:T(4,128)S(1)} all-gather(f32[1,4,5,256]{3,1,2,0:T(4,128)S(1)} %pad_maximum_fusion.8), channel_id=1, replica_groups=mesh['tile'=32,'lev'=8] {'tile'}, dimensions={0}, use_global_device_ids=true | all-gather | bytes 675840 | tf_op jit(solution)/shard_map/while/body/eval_jaxpr/all_gather | solution.py:63
  184.1 3.6 fusion.52
  187.6 12.6 %fusion.53 = f32[1,5,256,256]{3,0,2,1:T(1,128)S(1)} fusion(f32[1,5,256,256]{3,0,2,1:T(1,128)S(1)} %get-tuple-element.217, f32[1,5,1,256]{3,0,2,1:T(1,128)S(1)} %get-tuple-element.198, f32[1,5,255,256]{3,0,2,1:T(1,128)S(1)} %get-tuple-element.199, f32[1,5,255,256]{3,0,2,1:T(1,128)S(1)} %get-tuple-element.200, ...), kind=kLoop, calls=%fused_computation.13.clone.1 | loop fusion | flops 5242880 | bytes 8912896 | tf_op jit(solution)/shard_map/while/body/eval_jaxpr/add | solution.py:42
  200.4 3.3 copy.146
  203.7 23.0 %all_gather.12 = f32[32,4,5,256]{3,1,2,0:T(4,128)S(1)} all-gather(f32[1,4,5,256]{3,1,2,0:T(4,128)S(1)} %pad_maximum_fusion.8), channel_id=1, replica_groups=mesh['tile'=32,'lev'=8] {'tile'}, dimensions={0}, use_global_device_ids=true | all-gather | bytes 675840 | tf_op jit(solution)/shard_map/while/body/eval_jaxpr/all_gather | solution.py:63
  229.9 3.6 fusion.52
  233.5 12.6 %fusion.53 = f32[1,5,256,256]{3,0,2,1:T(1,128)S(1)} fusion(f32[1,5,256,256]{3,0,2,1:T(1,128)S(1)} %get-tuple-element.217, f32[1,5,1,256]{3,0,2,1:T(1,128)S(1)} %get-tuple-element.198, f32[1,5,255,256]{3,0,2,1:T(1,128)S(1)} %get-tuple-element.199, f32[1,5,255,256]{3,0,2,1:T(1,128)S(1)} %get-tuple-element.200, ...), kind=kLoop, calls=%fused_computation.13.clone.1 | loop fusion | flops 5242880 | bytes 8912896 | tf_op jit(solution)/shard_map/while/body/eval_jaxpr/add | solution.py:42
  246.2 3.3 copy.146
  249.5 23.9 %all_gather.12 = f32[32,4,5,256]{3,1,2,0:T(4,128)S(1)} all-gather(f32[1,4,5,256]{3,1,2,0:T(4,128)S(1)} %pad_maximum_fusion.8), channel_id=1, replica_groups=mesh['tile'=32,'lev'=8] {'tile'}, dimensions={0}, use_global_device_ids=true | all-gather | bytes 675840 | tf_op jit(solution)/shard_map/while/body/eval_jaxpr/all_gather | solution.py:63
  276.7 3.6 fusion.52
  280.3 12.6 %fusion.53 = f32[1,5,256,256]{3,0,2,1:T(1,128)S(1)} fusion(f32[1,5,256,256]{3,0,2,1:T(1,128)S(1)} %get-tuple-element.217, f32[1,5,1,256]{3,0,2,1:T(1,128)S(1)} %get-tuple-element.198, f32[1,5,255,256]{3,0,2,1:T(1,128)S(1)} %get-tuple-element.199, f32[1,5,255,256]{3,0,2,1:T(1,128)S(1)} %get-tuple-element.200, ...), kind=kLoop, calls=%fused_computation.13.clone.1 | loop fusion | flops 5242880 | bytes 8912896 | tf_op jit(solution)/shard_map/while/body/eval_jaxpr/add | solution.py:42
  293.0 3.3 copy.146
  296.4 22.8 %all_gather.12 = f32[32,4,5,256]{3,1,2,0:T(4,128)S(1)} all-gather(f32[1,4,5,256]{3,1,2,0:T(4,128)S(1)} %pad_maximum_fusion.8), channel_id=1, replica_groups=mesh['tile'=32,'lev'=8] {'tile'}, dimensions={0}, use_global_device_ids=true | all-gather | bytes 675840 | tf_op jit(solution)/shard_map/while/body/eval_jaxpr/all_gather | solution.py:63
  322.5 3.6 fusion.52
  326.1 12.6 %fusion.53 = f32[1,5,256,256]{3,0,2,1:T(1,128)S(1)} fusion(f32[1,5,256,256]{3,0,2,1:T(1,128)S(1)} %get-tuple-element.217, f32[1,5,1,256]{3,0,2,1:T(1,128)S(1)} %get-tuple-element.198, f32[1,5,255,256]{3,0,2,1:T(1,128)S(1)} %get-tuple-element.199, f32[1,5,255,256]{3,0,2,1:T(1,128)S(1)} %get-tuple-element.200, ...), kind=kLoop, calls=%fused_computation.13.clone.1 | loop fusion | flops 5242880 | bytes 8912896 | tf_op jit(solution)/shard_map/while/body/eval_jaxpr/add | solution.py:42
  338.8 3.3 copy.146
  342.1 24.0 %all_gather.12 = f32[32,4,5,256]{3,1,2,0:T(4,128)S(1)} all-gather(f32[1,4,5,256]{3,1,2,0:T(4,128)S(1)} %pad_maximum_fusion.8), channel_id=1, replica_groups=mesh['tile'=32,'lev'=8] {'tile'}, dimensions={0}, use_global_device_ids=true | all-gather | bytes 675840 | tf_op jit(solution)/shard_map/while/body/eval_jaxpr/all_gather | solution.py:63
  369.4 3.6 fusion.52
  373.0 12.6 %fusion.53 = f32[1,5,256,256]{3,0,2,1:T(1,128)S(1)} fusion(f32[1,5,256,256]{3,0,2,1:T(1,128)S(1)} %get-tuple-element.217, f32[1,5,1,256]{3,0,2,1:T(1,128)S(1)} %get-tuple-element.198, f32[1,5,255,256]{3,0,2,1:T(1,128)S(1)} %get-tuple-element.199, f32[1,5,255,256]{3,0,2,1:T(1,128)S(1)} %get-tuple-element.200, ...), kind=kLoop, calls=%fused_computation.13.clone.1 | loop fusion | flops 5242880 | bytes 8912896 | tf_op jit(solution)/shard_map/while/body/eval_jaxpr/add | solution.py:42
  385.7 3.3 copy.146
  389.0 22.8 %all_gather.12 = f32[32,4,5,256]{3,1,2,0:T(4,128)S(1)} all-gather(f32[1,4,5,256]{3,1,2,0:T(4,128)S(1)} %pad_maximum_fusion.8), channel_id=1, replica_groups=mesh['tile'=32,'lev'=8] {'tile'}, dimensions={0}, use_global_device_ids=true | all-gather | bytes 675840 | tf_op jit(solution)/shard_map/while/body/eval_jaxpr/all_gather | solution.py:63
  415.1 3.6 fusion.52
  418.6 12.6 %fusion.53 = f32[1,5,256,256]{3,0,2,1:T(1,128)S(1)} fusion(f32[1,5,256,256]{3,0,2,1:T(1,128)S(1)} %get-tuple-element.217, f32[1,5,1,256]{3,0,2,1:T(1,128)S(1)} %get-tuple-element.198, f32[1,5,255,256]{3,0,2,1:T(1,128)S(1)} %get-tuple-element.199, f32[1,5,255,256]{3,0,2,1:T(1,128)S(1)} %get-tuple-element.200, ...), kind=kLoop, calls=%fused_computation.13.clone.1 | loop fusion | flops 5242880 | bytes 8912896 | tf_op jit(solution)/shard_map/while/body/eval_jaxpr/add | solution.py:42
  431.4 3.3 copy.146
  434.7 24.1 %all_gather.12 = f32[32,4,5,256]{3,1,2,0:T(4,128)S(1)} all-gather(f32[1,4,5,256]{3,1,2,0:T(4,128)S(1)} %pad_maximum_fusion.8), channel_id=1, replica_groups=mesh['tile'=32,'lev'=8] {'tile'}, dimensions={0}, use_global_device_ids=true | all-gather | bytes 675840 | tf_op jit(solution)/shard_map/while/body/eval_jaxpr/all_gather | solution.py:63
  462.0 3.6 fusion.52
  465.6 12.6 %fusion.53 = f32[1,5,256,256]{3,0,2,1:T(1,128)S(1)} fusion(f32[1,5,256,256]{3,0,2,1:T(1,128)S(1)} %get-tuple-element.217, f32[1,5,1,256]{3,0,2,1:T(1,128)S(1)} %get-tuple-element.198, f32[1,5,255,256]{3,0,2,1:T(1,128)S(1)} %get-tuple-element.199, f32[1,5,255,256]{3,0,2,1:T(1,128)S(1)} %get-tuple-element.200, ...), kind=kLoop, calls=%fused_computation.13.clone.1 | loop fusion | flops 5242880 | bytes 8912896 | tf_op jit(solution)/shard_map/while/body/eval_jaxpr/add | solution.py:42
  478.3 3.3 copy.146
  481.7 22.7 %all_gather.12 = f32[32,4,5,256]{3,1,2,0:T(4,128)S(1)} all-gather(f32[1,4,5,256]{3,1,2,0:T(4,128)S(1)} %pad_maximum_fusion.8), channel_id=1, replica_groups=mesh['tile'=32,'lev'=8] {'tile'}, dimensions={0}, use_global_device_ids=true | all-gather | bytes 675840 | tf_op jit(solution)/shard_map/while/body/eval_jaxpr/all_gather | solution.py:63
  507.6 3.6 fusion.52
  511.2 12.6 %fusion.53 = f32[1,5,256,256]{3,0,2,1:T(1,128)S(1)} fusion(f32[1,5,256,256]{3,0,2,1:T(1,128)S(1)} %get-tuple-element.217, f32[1,5,1,256]{3,0,2,1:T(1,128)S(1)} %get-tuple-element.198, f32[1,5,255,256]{3,0,2,1:T(1,128)S(1)} %get-tuple-element.199, f32[1,5,255,256]{3,0,2,1:T(1,128)S(1)} %get-tuple-element.200, ...), kind=kLoop, calls=%fused_computation.13.clone.1 | loop fusion | flops 5242880 | bytes 8912896 | tf_op jit(solution)/shard_map/while/body/eval_jaxpr/add | solution.py:42
  524.1 2.0 convert_element_type.7
  526.1 116.2 %all-gather.2.cloned.1.call-done = bf16[1,40,65536]{2,0,1:T(2,128)(2,1)} async-done(((bf16[1,5,65536]{2,0,1:T(2,128)(2,1)}), bf16[1,40,65536]{2,0,1:T(2,128)(2,1)}) %all-gather.2.cloned.1.call-update) | async-done | bytes 5242896 | tf_op jit(solution)/shard_map/all_gather | solution.py:80
  642.3 9.6 %fusion.9 = f32[65536,5]{0,1:T(8,128)S(1)} fusion(bf16[1,40,65536]{2,0,1:T(2,128)(2,1)} %all-gather.2.cloned.1.call-done, bf16[40,40]{1,0:T(8,128)(2,1)S(1)} %copy-done, s32[]{:T(128)S(6)} %select_n.86), kind=kOutput, calls=%fused_computation.30 | convolution fusion | flops 26214400 | bytes 6555652 | tf_op jit(solution)/shard_map/kr,frn->fkn/dot_general | solution.py:77
  (191 shorter events, 52.8 us)
Async XLA Ops:
  6.5 635.8 %copy-start = (bf16[40,40]{1,0:T(8,128)(2,1)S(1)}, bf16[40,40]{1,0:T(8,128)(2,1)}, u32[]{:S(2)}) copy-start(bf16[40,40]{1,0:T(8,128)(2,1)} %param.13) | copy-start | bytes 9604
  6.5 635.8 %all-gather.2.cloned.1.call-start = ((), (), s32[]{:S(2)}) async-start(), calls=%async_computation | async-start | bytes 11796480 | tf_op jit(solution)/shard_map/all_gather | solution.py:80
  58.0 1.4 copy-start.1
  58.0 1.4 copy-start.2
  59.4 1.4 copy-start.3
  59.4 1.4 copy-start.4
Sparse Core Ops, SparseCore 0:
  526.2 116.0 all-gather.1
where the time goes:
time: 663 us; the launch traced here: 660 us
  blocking collectives  258 us (39%)
  other arithmetic  141 us (21%)
  local copies, waits for them, and re-layouts  120 us (18%)
  waiting for transfers between devices  116 us (17%)
  between operations  13.5 us (2%)
  matrix products  9.6 us (1%)
    all_gather x11, blocking collectives, rims_of(): lax.all_gather(tile_faces, 'tile', axis=0, tiled=True).reshape(flat_shape)  258 us
    add x10, other arithmetic, diffuse(): current + (to_west * (west_cells - current) + to_east * (east_cells - cur...  126 us
    all_gather x1, waiting for transfers between devices, shards(): lax.all_gather(smooth, 'lev', axis=1, tiled=True)  116 us
    slice x10, local copies, waits for them, and re-layouts, neighbours(): values[..., :, :-1]  35.8 us
    another operation x10, local copies, waits for them, and re-layouts  32.6 us
    slice x10, local copies, waits for them, and re-layouts, neighbours(): values[..., :-1, :]  13.5 us
  transfers between devices with their start and end apart: 1, of which 1 were waited for; matrix products, arithmetic and copies ran while one was open for 0% of the time, Pallas kernels for 0%

commit v1 on v0

v1 whole, which is shorter than its diff:
```python
import jax
import jax.numpy as jnp
from jax import lax
from jax.experimental import pallas as pl
from jax.experimental.pallas import tpu as pltpu
from jax.sharding import PartitionSpec as P

STEPS = 10
LEV = 5
PLANES = LEV + 3
SIDE = 256
ROWS = 32
HALO = 12
DEPTH = 10
STRIP = ROWS + DEPTH
TOP = 24
NORTH = 5
CHUNKS = 8

VMEM = pl.BlockSpec(memory_space=pltpu.VMEM)
SMEM = pl.BlockSpec(memory_space=pltpu.SMEM)


def lanes():
    return lax.broadcasted_iota(jnp.int32, (8, 128), 1)


def sublanes():
    return lax.broadcasted_iota(jnp.int32, (8, 128), 0)


def roll(x, shift):
    shift = shift % 128
    return x if shift == 0 else pltpu.roll(x, shift, 1)


def up(x):
    return pltpu.roll(x, 7, 0)


def down(x):
    return pltpu.roll(x, 1, 0)


def strided(halves, lead, t, half, stride):
    return halves[half][(*lead, pl.ds(t, 8, stride=stride), slice(None))]


def half_specs(*leads):
    return [
        pl.BlockSpec((*lead, SIDE, 128), lambda i, n=len(lead), h=h: (0,) * (n + 1) + (h,))
        for lead in leads
        for h in range(2)
    ]


def doubled(*arrays):
    return [a for a in arrays for _ in range(2)]


def paired(refs):
    return [refs[i : i + 2] for i in range(0, len(refs), 2)]


def planes_at(field, kx, ky, sea, t, half):
    land = strided(sea, (), t, half, ROWS).astype(jnp.float32)
    out = [strided(field, (l,), t, half, ROWS) * land for l in range(LEV)]
    return out + [land, strided(kx, (), t, half, ROWS), strided(ky, (), t, half, ROWS)]


def pack_kernel(links, *refs):
    field, kx, ky, sea = paired(refs[:8])
    west, east, north, nw, ne, rows = refs[8:]
    lane = lanes()
    group = lane // 16
    for t in range(ROWS):
        low = planes_at(field, kx, ky, sea, t, 0)
        high = planes_at(field, kx, ky, sea, t, 1)
        w, e = low[0], roll(high[0], 16)
        for p in range(1, PLANES):
            w = jnp.where(group == p, roll(low[p], 16 * p), w)
            e = jnp.where(group == p, roll(high[p], 16 * p + 16), e)
        west[8 * t : 8 * t + 8, :] = w
        east[8 * t : 8 * t + 8, :] = e
    flip = 127 - lane
    for p in range(PLANES):
        for o in range(2):
            for half in range(2):
                at = pl.ds(SIDE - 16 + 8 * o, 8)
                if p <= LEV:
                    x = sea[half][at, :].astype(jnp.float32)
                    x = field[half][p, at, :] * x if p < LEV else x
                else:
                    x = (kx, ky)[p - LEV - 1][half][at, :]
                x = jnp.take_along_axis(x, flip, axis=1)
                rows[p, 8 * o : 8 * o + 8, 128 * (1 - half) : 128 * (1 - half) + 128] = x
    for k in range(16):
        north[:, k, :] = rows[:, 15 - k, :]
    west_open = jnp.where(links[0, 0] >= 0, 1.0, 0.0).astype(jnp.float32)
    east_open = jnp.where(links[0, 1] >= 0, 1.0, 0.0).astype(jnp.float32)
    north[LEV, 14, :] = jnp.full((SIDE,), 1.0, jnp.float32) * west_open
    north[LEV, 15, :] = jnp.full((SIDE,), 1.0, jnp.float32) * east_open
    swap = jnp.bitwise_xor(lane, 15)
    for k in range(16):
        r = 8 * (ROWS - 1 - k) + 7
        nw[k : k + 1, :] = west[r : r + 1, :]
        ne[k : k + 1, :] = east[r : r + 1, :]
    for o in range(2):
        nw[8 * o : 8 * o + 8, :] = jnp.take_along_axis(nw[8 * o : 8 * o + 8, :], swap, axis=1)
        ne[8 * o : 8 * o + 8, :] = jnp.take_along_axis(ne[8 * o : 8 * o + 8, :], swap, axis=1)


def pack(links, field, kx, ky, sea):
    f32 = jnp.float32
    shapes = [(SIDE, 128), (SIDE, 128), (PLANES, 16, SIDE), (16, 128), (16, 128)]
    return pl.pallas_call(
        pack_kernel,
        out_shape=[jax.ShapeDtypeStruct(s, f32) for s in shapes],
        grid=(1,),
        in_specs=[SMEM] + half_specs((LEV,), (), (), ()),
        out_specs=[VMEM] * 5,
        scratch_shapes=[pltpu.VMEM((PLANES, 16, SIDE), f32)],
        compiler_params=pltpu.CompilerParams(vmem_limit_bytes=60 << 20),
        name="pack",
    )(links, *doubled(field, kx, ky, sea))


def wide_weights(sea, kx, ky, rows, we, ww, wn):
    lane, sub = lanes(), sublanes()
    for t in range(rows):
        s = [sea(t, h) for h in range(2)]
        x = [kx(t, h) for h in range(2)]
        se = [jnp.where(lane == 127, roll(s[1], -1), roll(s[0], -1)), roll(s[1], -1)]
        xe = [jnp.where(lane == 127, roll(x[1], -1), roll(x[0], -1)), roll(x[1], -1)]
        shifted = []
        for h in range(2):
            w = 0.5 * (x[h] + xe[h]) * s[h] * se[h]
            if h == 1:
                w = jnp.where(lane == 127, 0.0, w)
            we[t, :, 128 * h : 128 * h + 128] = w
            shifted.append(roll(w, 1))
            if t < rows - 1:
                sn, yn = sea(t + 1, h), ky(t + 1, h)
            else:
                sn, yn = up(sea(0, h)), up(ky(0, h))
            w = 0.5 * (ky(t, h) + yn) * s[h] * sn
            if t == rows - 1:
                w = jnp.where(sub == 7, 0.0, w)
            wn[t, :, 128 * h : 128 * h + 128] = w
        ww[t, :, 0:128] = jnp.where(lane == 0, 0.0, shifted[0])
        ww[t, :, 128:256] = jnp.where(lane == 0, shifted[0], shifted[1])


HALVES = (slice(0, 128), slice(128, 256))


def wide_step(src, dst, we, ww, wn, rows, levels, block):
    lane = lanes()
    first, last = lane == 0, lane == 127
    below = []
    for l in levels:
        for h in HALVES:
            over = up(src[l, 0, :, h])
            src[l, rows, :, h] = over
            below.append(down(wn[rows - 1, :, h] * (over - src[l, rows - 1, :, h])))

    def body(b, below):
        here = [src[l, b * block, :, h] for l in levels for h in HALVES]
        for j in range(block):
            t = b * block + j
            e = [we[t, :, h] for h in HALVES]
            w = [ww[t, :, h] for h in HALVES]
            n = [wn[t, :, h] for h in HALVES]
            nxt = [src[l, t + 1, :, h] for l in levels for h in HALVES]
            flux = [n[i % 2] * (nxt[i] - here[i]) for i in range(len(here))]
            for i, l in zip(range(0, len(here), 2), levels):
                lo, hi = here[i : i + 2]
                e_lo, e_hi = roll(lo, -1), roll(hi, -1)
                w_lo, w_hi = roll(lo, 1), roll(hi, 1)
                x_lo = e[0] * (jnp.where(last, e_hi, e_lo) - lo) + w[0] * (w_lo - lo)
                x_hi = e[1] * (e_hi - hi) + w[1] * (jnp.where(first, w_lo, w_hi) - hi)
                dst[l, t, :, HALVES[0]] = lo + x_lo + (flux[i] - below[i])
                dst[l, t, :, HALVES[1]] = hi + x_hi + (flux[i + 1] - below[i + 1])
            here, below = nxt, flux
        return tuple(below)

    if rows == block:
        body(0, below)
    else:
        lax.fori_loop(0, rows // block, body, tuple(below))


def mixing(vertical):
    levels = vertical.shape[0]
    size = 16 * levels

    def at(shape, axis):
        return lax.broadcasted_iota(jnp.int32, shape, axis)

    left = (at((size, levels), 0) // 16 == at((size, levels), 1)).astype(jnp.float32).astype(jnp.bfloat16)
    right = (at((levels, size), 1) // 16 == at((levels, size), 0)).astype(jnp.float32).astype(jnp.bfloat16)
    tall = jnp.dot(left, vertical, preferred_element_type=jnp.float32).astype(jnp.bfloat16)
    full = jnp.dot(tall, right, preferred_element_type=jnp.float32)
    same = at((size, size), 0) % 16 == at((size, size), 1) % 16
    return jnp.where(same, full, 0.0).astype(jnp.bfloat16)


def inner_kernel(*refs):
    field, kx, ky, sea = paired(refs[:8])
    vertical, cur, own, statics, top, mixer, other, we, ww, wn = refs[8:]
    lane = lanes()
    group = lane // 32

    def plane(ref):
        return lambda t, h: strided(ref, (), t, h, ROWS).astype(jnp.float32)

    wide_weights(plane(sea), plane(kx), plane(ky), ROWS, we, ww, wn)
    for t in range(ROWS):
        low = planes_at(field, kx, ky, sea, t, 0)
        high = planes_at(field, kx, ky, sea, t, 1)
        for l in range(LEV):
            cur[l, t, :, 0:128] = low[l]
            cur[l, t, :, 128:256] = high[l]
        a, b = roll(low[0], HALO), roll(high[0], -108)
        for l in range(1, 4):
            a = jnp.where(group == l, roll(low[l], HALO + 32 * l), a)
            b = jnp.where(group == l, roll(high[l], 32 * l - 108), b)
        own[0, t] = a
        own[1, t] = b
        own[2, t] = jnp.where(group == 0, roll(low[4], HALO), roll(high[4], 32 - 108))
        for p in range(3):
            statics[p, t] = jnp.where(group == 0, roll(low[LEV + p], HALO), roll(high[LEV + p], 32 - 108))
    for h in range(2):
        land = sea[h][SIDE - TOP :, :].astype(jnp.float32)
        for l in range(LEV):
            top[h, l] = field[h][l, SIDE - TOP :, :] * land
        top[h, LEV] = land
        top[h, LEV + 1] = kx[h][SIDE - TOP :, :]
        top[h, LEV + 2] = ky[h][SIDE - TOP :, :]

    mixer[...] = mixing(vertical[...])

    def two_steps(_, none):
        wide_step(cur, other, we, ww, wn, ROWS, range(LEV), 8)
        wide_step(other, cur, we, ww, wn, ROWS, range(LEV), 8)
        return none

    lax.fori_loop(0, STEPS // 2, two_steps, 0)


def inner(field, kx, ky, sea, vertical):
    f32 = jnp.float32
    shapes = [(LEV, ROWS + 1, 8, SIDE), (3, ROWS, 8, 128), (3, ROWS, 8, 128), (2, PLANES, TOP, 128)]
    return pl.pallas_call(
        inner_kernel,
        out_shape=[jax.ShapeDtypeStruct(s, f32) for s in shapes] + [jax.ShapeDtypeStruct((640, 640), jnp.bfloat16)],
        grid=(1,),
        in_specs=half_specs((LEV,), (), (), ()) + [VMEM],
        out_specs=[VMEM] * 5,
        scratch_shapes=[pltpu.VMEM((LEV, ROWS + 1, 8, SIDE), f32)] + [pltpu.VMEM((ROWS, 8, SIDE), f32)] * 3,
        compiler_params=pltpu.CompilerParams(vmem_limit_bytes=24 << 20),
        cost_estimate=pl.CostEstimate(flops=40_000_000, bytes_accessed=40_000_000, transcendentals=0),
        name="inner",
    )(*doubled(field, kx, ky, sea), vertical)


def strip_step(src, dst, we, ww, wn, tiles, block):
    sub = sublanes()
    below = []
    for k in tiles:
        over = jnp.where(sub == 7, src[k, ROWS], up(src[k, 0]))
        src[k, ROWS] = over
        below.append(jnp.where(sub == 0, 0.0, down(wn[k, ROWS - 1] * (over - src[k, ROWS - 1]))))

    def body(b, below):
        here = [src[k, b * block] for k in tiles]
        for j in range(block):
            t = b * block + j
            nxt = [src[k, t + 1] for k in tiles]
            flux = [wn[k, t] * (n - c) for k, n, c in zip(tiles, nxt, here)]
            for k, c, f, g in zip(tiles, here, flux, below):
                x = we[k, t] * (roll(c, -1) - c) + ww[k, t] * (roll(c, 1) - c)
                dst[k, t] = c + x + (f - g)
            here, below = nxt, flux
        return tuple(below)

    lax.fori_loop(0, STRIP // block, body, tuple(below))


def rim_kernel(links, inside, own, statics, top, west, east, north, nw, ne, out, cur, other, we, ww, wn, nb_west, nb_east, nc, n_other, nwe, nww, nwn, st):
    lane, sub = lanes(), sublanes()
    group, part = lane // 32, lane % 32
    w_halo, e_halo = part < HALO, part >= 20
    ones = jnp.ones((8, 128), jnp.float32)

    for t in range(STRIP):
        if t < ROWS:
            w, e = west[8 * t : 8 * t + 8, :], east[8 * t : 8 * t + 8, :]
            a, b, c = own[0, t], own[1, t], own[2, t]
            s = [statics[p, t] for p in range(3)]
        else:
            k = t - ROWS
            w = jnp.broadcast_to(nw[k : k + 1, :], (8, 128))
            e = jnp.broadcast_to(ne[k : k + 1, :], (8, 128))
            low = [jnp.broadcast_to(north[p, k : k + 1, 0:128], (8, 128)) for p in range(PLANES)]
            high = [jnp.broadcast_to(north[p, k : k + 1, 128:256], (8, 128)) for p in range(PLANES)]
            a, b = roll(low[0], HALO), roll(high[0], -108)
            for l in range(1, 4):
                a = jnp.where(group == l, roll(low[l], HALO + 32 * l), a)
                b = jnp.where(group == l, roll(high[l], 32 * l - 108), b)
            c = jnp.where(group == 0, roll(low[4], HALO), roll(high[4], 32 - 108))
            s = [jnp.where(group == 0, roll(low[LEV + p], HALO), roll(high[LEV + p], 32 - 108)) for p in range(3)]
        for l in range(4):
            a = jnp.where(w_halo & (group == l), roll(w, 16 * l - 4), a)
            b = jnp.where(e_halo & (group == l), roll(e, 16 * l + 20), b)
        c = jnp.where(w_halo & (group == 0), roll(w, -68), c)
        c = jnp.where(e_halo & (group == 1), roll(e, 52 - 64), c)
        cur[0, t] = a
        cur[1, t] = b
        cur[2, t] = c
        for p in range(3):
            q = LEV + p
            x = jnp.where(w_halo & (group == 0), roll(w, -(16 * q + 4)), s[p])
            st[p, t] = jnp.where(e_halo & (group == 1), roll(e, 52 - 16 * q), x)

    def flag(x):
        return jnp.where(x >= 0, 1.0, 0.0).astype(jnp.float32)

    w_open = ones * flag(links[0, 0])
    e_open = ones * flag(links[0, 1])
    w_over = jnp.broadcast_to(north[LEV, 15:16, 0:128], (8, 128))
    e_over = jnp.broadcast_to(north[LEV, 14:15, 0:128], (8, 128))
    shut = part == 31
    w_seam, e_seam = lane == HALO - 1, lane == 32 + 19
    seams = []
    for a, b in ((w_open, e_open), (w_over, e_over)):
        m = jnp.where(w_seam, a, jnp.where(e_seam, b, 1.0))
        seams.append(0.5 * jnp.where(shut, 0.0, m))

    def spread(x):
        lo = jnp.where(group == 0, x, 0.0)
        hi = jnp.where(group == 1, x, 0.0)
        lo = lo + roll(lo, 32)
        hi = hi + roll(hi, 32)
        return lo + roll(lo, 64), hi + roll(hi, 64)

    for t in range(STRIP):
        s, x, y = st[0, t], st[1, t], st[2, t]
        w = seams[t >= ROWS] * (x + roll(x, -1)) * s * roll(s, -1)
        we[0, t], we[1, t] = spread(w)
        we[2, t] = w
        for i in range(3):
            ww[i, t] = roll(we[i, t], 1)
        if t < STRIP - 1:
            sn, yn = st[0, t + 1], st[2, t + 1]
            if t == ROWS - 1:
                sn = jnp.where(sub == 7, sn, up(st[0, 0]))
                yn = jnp.where(sub == 7, yn, up(st[2, 0]))
            w = 0.5 * (y + yn) * s * sn
            wn[0, t], wn[1, t] = spread(w)
            wn[2, t] = w

    zeros = jnp.zeros((8, 128), jnp.float32)
    for i in range(3):
        wn[i, STRIP - 1] = zeros
        cur[i, STRIP] = zeros
        other[i, STRIP] = zeros

    nb = (nb_west, nb_east)
    for h in range(2):
        nb[h][:, 0:TOP, :] = top[h]
        nb[h][:, TOP : TOP + 16, :] = north[:, :, 128 * h : 128 * h + 128]
    for l in range(LEV):
        for t in range(NORTH):
            for h in range(2):
                nc[l, t, :, 128 * h : 128 * h + 128] = strided(nb, (l,), t, h, NORTH)

    def plane(p):
        return lambda t, h: strided(nb, (p,), t, h, NORTH)

    wide_weights(plane(LEV), plane(LEV + 1), plane(LEV + 2), NORTH, nwe, nww, nwn)

    def two_steps(_, none):
        strip_step(cur, other, we, ww, wn, range(3), 14)
        wide_step(nc, n_other, nwe, nww, nwn, NORTH, range(LEV), NORTH)
        strip_step(other, cur, we, ww, wn, range(3), 14)
        wide_step(n_other, nc, nwe, nww, nwn, NORTH, range(LEV), NORTH)
        return none

    lax.fori_loop(0, STEPS // 2, two_steps, 0)

    for l in range(LEV):
        for t in range(NORTH):
            for h in range(2):
                nb[h][l, pl.ds(t, 8, stride=NORTH), :] = nc[l, t, :, 128 * h : 128 * h + 128]

    w_rim, e_rim = lane < 10, lane >= 118
    top_row = sub == 7
    for l in range(LEV):
        for t in range(0, ROWS, 2):
            pair = []
            for u in (t, t + 1):
                lo, hi = inside[l, u, :, 0:128], inside[l, u, :, 128:256]
                if u >= ROWS - DEPTH:
                    r = TOP - ROWS + u
                    lo = jnp.where(top_row, jnp.broadcast_to(nb[0][l, r : r + 1, :], (8, 128)), lo)
                    hi = jnp.where(top_row, jnp.broadcast_to(nb[1][l, r : r + 1, :], (8, 128)), hi)
                if l < 4:
                    w, e = roll(cur[0, u], -(32 * l + HALO)), roll(cur[1, u], 108 - 32 * l)
                else:
                    w, e = roll(cur[2, u], -HALO), roll(cur[2, u], 108 - 32)
                pair.append((jnp.where(w_rim, w, lo), jnp.where(e_rim, e, hi)))
            q, r = t // 4, 8 * (t % 4)
            for h in range(2):
                x = jnp.concatenate([pair[0][h], pair[1][h]], axis=0)
                out[q, l, r : r + 16, 128 * h : 128 * h + 128] = x.astype(jnp.bfloat16)


def rim(links, inside, own, statics, top, west, east, north, nw, ne):
    f32 = jnp.float32
    scratch = [
        (3, STRIP + 1, 8, 128),
        (3, STRIP + 1, 8, 128),
        (3, STRIP, 8, 128),
        (3, STRIP, 8, 128),
        (3, STRIP, 8, 128),
        (PLANES, TOP + 16, 128),
        (PLANES, TOP + 16, 128),
        (LEV, NORTH + 1, 8, SIDE),
        (LEV, NORTH + 1, 8, SIDE),
        (NORTH, 8, SIDE),
        (NORTH, 8, SIDE),
        (NORTH, 8, SIDE),
        (3, STRIP, 8, 128),
    ]
    return pl.pallas_call(
        rim_kernel,
        out_shape=jax.ShapeDtypeStruct((CHUNKS, LEV, SIDE // CHUNKS, SIDE), jnp.bfloat16),
        in_specs=[SMEM] + [VMEM] * 9,
        out_specs=VMEM,
        scratch_shapes=[pltpu.VMEM(s, f32) for s in scratch],
        compiler_params=pltpu.CompilerParams(vmem_limit_bytes=24 << 20),
        name="rim",
    )(links, inside, own, statics, top, west, east, north, nw, ne)


def mix_kernel(x, k, y):
    for h in range(2):
        rows = x[:, :, 16 * h : 16 * h + 16, :].reshape(CHUNKS * LEV * 16, SIDE)
        mixed = jnp.dot(k[...], rows, preferred_element_type=jnp.float32).astype(jnp.bfloat16)
        y[:, :, 16 * h : 16 * h + 16, :] = mixed.reshape(CHUNKS, LEV, 16, SIDE)


def mix(x, k):
    return pl.pallas_call(
        mix_kernel,
        out_shape=jax.ShapeDtypeStruct(x.shape, jnp.bfloat16),
        in_specs=[VMEM] * 2,
        out_specs=VMEM,
        compiler_params=pltpu.CompilerParams(vmem_limit_bytes=24 << 20),
        name="mix",
    )(x, k)


def unpack_kernel(z, out):
    for q in range(CHUNKS):
        for l in range(LEV):
            for r in range(0, 32, 16):
                x = z[q, l, r : r + 16, :].astype(jnp.float32)
                for u in range(2):
                    t = 4 * q + r // 8 + u
                    out[l, pl.ds(t, 8, stride=ROWS), :] = x[8 * u : 8 * u + 8]


def unpack(z):
    return pl.pallas_call(
        unpack_kernel,
        out_shape=jax.ShapeDtypeStruct((LEV, SIDE, SIDE), jnp.float32),
        grid=(2,),
        in_specs=[pl.BlockSpec((CHUNKS, LEV, SIDE // CHUNKS, 128), lambda h: (0, 0, 0, h))],
        out_specs=pl.BlockSpec((LEV, SIDE, 128), lambda h: (0, 0, h)),
        compiler_params=pltpu.CompilerParams(vmem_limit_bytes=24 << 20),
        name="unpack",
    )(z)


def shards(field, kappa_x, kappa_y, sea_mask, tile_links, vertical):
    tiles = lax.axis_size("tile")

    def send(x, target):
        return lax.ppermute(x, "tile", [(i, target(i) % tiles) for i in range(tiles)])

    cells, kx, ky, sea = field[0], kappa_x[0], kappa_y[0], sea_mask[0]
    west, east, north, nw, ne = pack(tile_links, cells, kx, ky, sea)
    from_east = send(west, lambda i: i - 1)
    from_west = send(east, lambda i: i + 1)
    from_north = send(north, lambda i: -i)
    from_nw = send(nw, lambda i: 1 - i)
    from_ne = send(ne, lambda i: -1 - i)
    inside, own, statics, top, mixer = inner(cells, kx, ky, sea, vertical)
    smooth = rim(tile_links, inside, own, statics, top, from_west, from_east, from_north, from_nw, from_ne)
    gathered = lax.all_to_all(smooth, "lev", 0, 0, tiled=True)
    back = lax.all_to_all(mix(gathered, mixer), "lev", 0, 0, tiled=True)
    return unpack(back)[None]


def solution(mesh):
    placed = (
        P("tile", "lev", None, None),
        P("tile", None, None),
        P("tile", None, None),
        P("tile", None, None),
        P("tile", None),
        P(),
    )
    return jax.shard_map(
        shards, mesh=mesh, in_specs=placed, out_specs=P("tile", "lev", None, None), check_vma=False
    )
```

time: 663 us -> 100 us (0.15)
  blocking collectives: 258 us -> 51.9 us
  other arithmetic: 141 us -> 0 us
  local copies, waits for them, and re-layouts: 120 us -> 0.02 us
  waiting for transfers between devices: 116 us -> 0.01 us
  Pallas kernels: 0 us -> 38.3 us
  between operations: 13.5 us -> 0.13 us
  starting transfers between devices: 0.01 us -> 9.65 us
  matrix products: 9.6 us -> 0 us
    all_gather x11 -> x0, blocking collectives: 258 us -> none  [rims_of(): lax.all_gather(tile_faces, 'tile', axis=0, tiled=True).reshape(flat_shape)]
    add x10 -> x0, other arithmetic: 126 us -> none  [diffuse(): current + (to_west * (west_cells - current) + to_east * (east_cells - cur...]
    all_gather x1 -> x0, waiting for transfers between devices: 116 us -> none  [shards(): lax.all_gather(smooth, 'lev', axis=1, tiled=True)]
    slice x23 -> x0, local copies, waits for them, and re-layouts: 56.8 us -> none  [the longest x10 35.8 us: neighbours(): values[..., :, :-1]]
    all_to_all x0 -> x2, blocking collectives: none -> 51.9 us  [the longest x1 28.8 us: shards(): gathered = lax.all_to_all(smooth, 'lev', 0, 0, tiled=True)]
    another operation x19 -> x0, local copies, waits for them, and re-layouts: 39.2 us -> none
    pallas_call x0 -> x5, Pallas kernels: none -> 38.3 us  [the longest x1 18.5 us: rim(): pl.pallas_call(rim_kernel, out_shape=jax.ShapeDtypeStruct((CHUNKS, LEV, S...]
    ppermute x0 -> x5, starting transfers between devices: none -> 9.65 us  [send(): lax.ppermute(x, 'tile', [(i, target(i) % tiles) for i in range(tiles)])]
  transfers between devices with their start and end apart: 1 -> 5, of which waited for: 1 -> 0; matrix products, arithmetic and copies ran while one was open for 0% -> 0% of each run, Pallas kernels for 0% -> 13%
where the time goes in v1:
time: 100 us
  blocking collectives  51.9 us (52%)
  Pallas kernels  38.3 us (38%)
  starting transfers between devices  9.65 us (10%)
    all_to_all x1, blocking collectives, shards(): gathered = lax.all_to_all(smooth, 'lev', 0, 0, tiled=True)  28.8 us
    all_to_all x1, blocking collectives, shards(): back = lax.all_to_all(mix(gathered, mixer), 'lev', 0, 0, tiled=True)  23.1 us
    pallas_call x1, Pallas kernels, rim(): pl.pallas_call(rim_kernel, out_shape=jax.ShapeDtypeStruct((CHUNKS, LEV, S...  18.5 us
    pallas_call x1, Pallas kernels, inner(): pl.pallas_call(inner_kernel, out_shape=[jax.ShapeDtypeStruct(s, f32) for...  13.5 us
    ppermute x5, starting transfers between devices, send(): lax.ppermute(x, 'tile', [(i, target(i) % tiles) for i in range(tiles)])  9.65 us
    pallas_call x1, Pallas kernels, pack(): pl.pallas_call(pack_kernel, out_shape=[jax.ShapeDtypeStruct(s, f32) for s...  3.89 us
  transfers between devices with their start and end apart: 5, of which 0 were waited for; matrix products, arithmetic and copies ran while one was open for 0% of the time, Pallas kernels for 13%

profile of v1, /device:TPU:15, one launch (start us, length us, event | category | flops | bytes accessed | tf_op | source)
XLA Modules:
  0.0 100.0 jit_solution(468569159002538186)
XLA Ops:
  0.0 0.0 copy-start
  0.0 0.0 copy-start.1
  0.0 0.0 copy-start.2
  0.0 0.0 copy-start.3
  0.0 0.0 copy-start.4
  0.0 3.9 %pack.1 = (f32[256,128]{1,0:T(8,128)}, f32[256,128]{1,0:T(8,128)}, f32[8,16,256]{2,1,0:T(8,128)}, f32[16,128]{1,0:T(8,128)}, f32[16,128]{1,0:T(8,128)}) custom-call(s32[1,4]{1,0:T(1,128)} %links.3, f32[5,256,256]{2,1,0:T(8,128)} %bitcast.5, f32[5,256,256]{2,1,0:T(8,128)} %bitcast.6, f32[256,256]{1,0:T(8,128)} %bitcast.9, f32[256,256]{1,0:T(8,128)} %bitcast.10, ...), custom_call_target="tpu_custom_call" | custom-call | tf_op jit(solution)/shard_map/pack/pallas_call | solution.py:116
  3.9 1.9 %collective-permute-start = (f32[256,128]{1,0:T(8,128)}, f32[256,128]{1,0:T(8,128)S(1)}, u32[]{:S(2)}, u32[]{:S(2)}) collective-permute-start(f32[256,128]{1,0:T(8,128)} %get-tuple-element.19), channel_id=1, source_target_pairs={{0,8},{8,16},{16,24},{24,32},{32,40},{40,48},{48,56},{56,64},{64,7... | collective-permute-start | bytes 393224 | tf_op jit(solution)/shard_map/ppermute | solution.py:491
  5.8 0.0 collective-permute-start.1
  5.8 2.8 %collective-permute-start.2 = (f32[8,16,256]{2,1,0:T(8,128)}, f32[8,16,256]{2,1,0:T(8,128)S(1)}, u32[]{:S(2)}, u32[]{:S(2)}) collective-permute-start(f32[8,16,256]{2,1,0:T(8,128)} %get-tuple-element.21), channel_id=1, source_target_pairs={{0,0},{8,248},{16,240},{24,232},{32,224},{40,216},{48,208},{56,200... | collective-permute-start | bytes 393224 | tf_op jit(solution)/shard_map/ppermute | solution.py:491
  8.6 5.0 %collective-permute-start.3 = (f32[16,128]{1,0:T(8,128)}, f32[16,128]{1,0:T(8,128)S(1)}, u32[]{:S(2)}, u32[]{:S(2)}) collective-permute-start(f32[16,128]{1,0:T(8,128)} %get-tuple-element.22), channel_id=1, source_target_pairs={{0,8},{8,0},{16,248},{24,240},{32,232},{40,224},{48,216},{56,208},... | collective-permute-start | bytes 24584 | tf_op jit(solution)/shard_map/ppermute | solution.py:491
  13.6 0.0 copy-start.5
  13.6 0.0 collective-permute-start.4
  13.6 0.0 copy-done
  13.6 0.0 copy-done.1
  13.6 0.0 copy-done.2
  13.6 0.0 copy-done.3
  13.6 0.0 copy-done.4
  13.6 13.5 %inner.1 = (f32[5,33,8,256]{3,2,1,0:T(8,128)S(1)}, f32[3,32,8,128]{3,2,1,0:T(8,128)S(1)}, f32[3,32,8,128]{3,2,1,0:T(8,128)S(1)}, f32[2,8,24,128]{3,2,1,0:T(8,128)S(1)}, bf16[640,640]{1,0:T(8,128)(2,1)S(1)}) custom-call(f32[5,256,256]{2,1,0:T(8,128)S(1)} %bitcast.7, f32[5,256,256]{2,1,0:T(8,128)S(1)} %bitcast.8, f32[256,256]{1,0:T(8,128)S(1)} %bitcast.11, ...), custom_call_target="tpu_custom_call" | custom-call | flops 40000000 | bytes 40000000 | tf_op jit(solution)/shard_map/inner/pallas_call | solution.py:254
  27.1 0.0 collective-permute-done.3.nw
  27.1 0.0 collective-permute-done.4.ne
  27.1 0.0 collective-permute-done.west
  27.1 0.0 collective-permute-done.1.east
  27.1 0.0 collective-permute-done.2.north
  27.1 0.0 copy-done.5
  27.1 18.5 %rim.1 = bf16[8,5,32,256]{3,2,1,0:T(8,128)(2,1)S(1)} custom-call(s32[1,4]{1,0:T(1,128)S(1)} %copy-done.5, f32[5,33,8,256]{3,2,1,0:T(8,128)S(1)} %get-tuple-element.15.inside, f32[3,32,8,128]{3,2,1,0:T(8,128)S(1)} %get-tuple-element.16.own, f32[3,32,8,128]{3,2,1,0:T(8,128)S(1)} %get-tuple-element.17.statics, f32[2,8,24,128]{3,2,1,0:T(8,128)S(1)} %get-tuple-element.18.top, ...), custom_call_target="tpu_custom_call" | custom-call | tf_op jit(solution)/shard_map/rim/pallas_call | solution.py:436
  45.7 28.8 %all_to_all.10.x = bf16[8,5,32,256]{3,2,1,0:T(8,128)(2,1)S(1)} all-to-all(bf16[8,5,32,256]{3,2,1,0:T(8,128)(2,1)S(1)} %rim.1), channel_id=1, replica_groups=mesh['tile'=32,'lev'=8] {'lev'}, dimensions={0} | all-to-all | bytes 1310720 | tf_op jit(solution)/shard_map/all_to_all | solution.py:502
  74.4 0.7 mix.1
  75.1 23.1 %all_to_all.11.z = bf16[8,5,32,256]{3,2,1,0:T(8,128)(2,1)S(1)} all-to-all(bf16[8,5,32,256]{3,2,1,0:T(8,128)(2,1)S(1)} %mix.1), channel_id=1, replica_groups=mesh['tile'=32,'lev'=8] {'lev'}, dimensions={0} | all-to-all | bytes 1310720 | tf_op jit(solution)/shard_map/all_to_all | solution.py:503
  98.2 1.8 %unpack.1 = f32[5,256,256]{2,1,0:T(8,128)} custom-call(bf16[8,5,32,256]{3,2,1,0:T(8,128)(2,1)S(1)} %all_to_all.11.z), custom_call_target="tpu_custom_call" | custom-call | tf_op jit(solution)/shard_map/unpack/pallas_call | solution.py:476
Async XLA Ops:
  0.0 13.6 %copy-start = (f32[1,5,256,256]{3,2,1,0:T(8,128)S(1)}, f32[1,5,256,256]{3,2,1,0:T(8,128)}, u32[]{:S(2)}) copy-start(f32[1,5,256,256]{3,2,1,0:T(8,128)} %param.6) | copy-start | bytes 3932164
  0.0 13.6 %copy-start.1 = (f32[1,256,256]{2,1,0:T(8,128)S(1)}, f32[1,256,256]{2,1,0:T(8,128)}, u32[]{:S(2)}) copy-start(f32[1,256,256]{2,1,0:T(8,128)} %param.7) | copy-start | bytes 786436
  0.0 13.6 %copy-start.2 = (f32[1,256,256]{2,1,0:T(8,128)S(1)}, f32[1,256,256]{2,1,0:T(8,128)}, u32[]{:S(2)}) copy-start(f32[1,256,256]{2,1,0:T(8,128)} %param.8) | copy-start | bytes 786436
  0.0 13.6 %copy-start.3 = (s32[1,256,256]{2,1,0:T(8,128)S(1)}, s32[1,256,256]{2,1,0:T(8,128)}, u32[]{:S(2)}) copy-start(s32[1,256,256]{2,1,0:T(8,128)} %param.9) | copy-start | bytes 786436
  0.0 13.6 %copy-start.4 = (bf16[40,40]{1,0:T(8,128)(2,1)S(1)}, bf16[40,40]{1,0:T(8,128)(2,1)}, u32[]{:S(2)}) copy-start(bf16[40,40]{1,0:T(8,128)(2,1)} %refs_8_.1) | copy-start | bytes 9604
  3.9 23.2 %collective-permute-start = (f32[256,128]{1,0:T(8,128)}, f32[256,128]{1,0:T(8,128)S(1)}, u32[]{:S(2)}, u32[]{:S(2)}) collective-permute-start(f32[256,128]{1,0:T(8,128)} %get-tuple-element.19), channel_id=1, source_target_pairs={{0,8},{8,16},{16,24},{24,32},{32,40},{40,48},{48,56},{56,64},{64,7... | collective-permute-start | bytes 393224 | tf_op jit(solution)/shard_map/ppermute | solution.py:491
  5.8 21.3 %collective-permute-start.1 = (f32[256,128]{1,0:T(8,128)}, f32[256,128]{1,0:T(8,128)S(1)}, u32[]{:S(2)}, u32[]{:S(2)}) collective-permute-start(f32[256,128]{1,0:T(8,128)} %get-tuple-element.20), channel_id=1, source_target_pairs={{0,248},{8,0},{16,8},{24,16},{32,24},{40,32},{48,40},{56,48},{64,5... | collective-permute-start | bytes 393224 | tf_op jit(solution)/shard_map/ppermute | solution.py:491
  5.8 21.4 %collective-permute-start.2 = (f32[8,16,256]{2,1,0:T(8,128)}, f32[8,16,256]{2,1,0:T(8,128)S(1)}, u32[]{:S(2)}, u32[]{:S(2)}) collective-permute-start(f32[8,16,256]{2,1,0:T(8,128)} %get-tuple-element.21), channel_id=1, source_target_pairs={{0,0},{8,248},{16,240},{24,232},{32,224},{40,216},{48,208},{56,200... | collective-permute-start | bytes 393224 | tf_op jit(solution)/shard_map/ppermute | solution.py:491
  8.6 18.5 %collective-permute-start.3 = (f32[16,128]{1,0:T(8,128)}, f32[16,128]{1,0:T(8,128)S(1)}, u32[]{:S(2)}, u32[]{:S(2)}) collective-permute-start(f32[16,128]{1,0:T(8,128)} %get-tuple-element.22), channel_id=1, source_target_pairs={{0,8},{8,0},{16,248},{24,240},{32,232},{40,224},{48,216},{56,208},... | collective-permute-start | bytes 24584 | tf_op jit(solution)/shard_map/ppermute | solution.py:491
  13.6 13.6 %copy-start.5 = (s32[1,4]{1,0:T(1,128)S(1)}, s32[1,4]{1,0:T(1,128)}, u32[]{:S(2)}) copy-start(s32[1,4]{1,0:T(1,128)} %links.3) | copy-start | bytes 52
  13.6 13.5 %collective-permute-start.4 = (f32[16,128]{1,0:T(8,128)}, f32[16,128]{1,0:T(8,128)S(1)}, u32[]{:S(2)}, u32[]{:S(2)}) collective-permute-start(f32[16,128]{1,0:T(8,128)} %get-tuple-element.23), channel_id=1, source_target_pairs={{0,248},{8,240},{16,232},{24,224},{32,216},{40,208},{48,200},{56,1... | collective-permute-start | bytes 24584 | tf_op jit(solution)/shard_map/ppermute | solution.py:491

commit v2 on v1

v2 whole, which is shorter than its diff:
```python
import jax
import jax.numpy as jnp
from jax import lax
from jax.experimental import pallas as pl
from jax.experimental.pallas import tpu as pltpu
from jax.sharding import PartitionSpec as P

STEPS = 10
LEV = 5
PLANES = LEV + 3
SIDE = 256
ROWS = 32
HALO = 12
DEPTH = 10
STRIP = ROWS + DEPTH
TOP = 24
NORTH = 5
CHUNKS = 8
SLOT = (0, 4, 2, 6, 1, 5, 3, 7)
TILES = ((0, 1), (2, 3), (4, 5), (6, 7))
W_SHIFT = (-4, -36, -20, -52)
E_SHIFT = (52, 20, 36, 4)

VMEM = pl.BlockSpec(memory_space=pltpu.VMEM)
SMEM = pl.BlockSpec(memory_space=pltpu.SMEM)


def lanes():
    return lax.broadcasted_iota(jnp.int32, (8, 128), 1)


def sublanes():
    return lax.broadcasted_iota(jnp.int32, (8, 128), 0)


def roll(x, shift):
    shift = shift % 128
    return x if shift == 0 else pltpu.roll(x, shift, 1)


def up(x):
    return pltpu.roll(x, 7, 0)


def down(x):
    return pltpu.roll(x, 1, 0)


def strided(halves, lead, t, half, stride):
    return halves[half][(*lead, pl.ds(t, 8, stride=stride), slice(None))]


def half_specs(*leads):
    return [
        pl.BlockSpec((*lead, SIDE, 128), lambda i, n=len(lead), h=h: (0,) * (n + 1) + (h,))
        for lead in leads
        for h in range(2)
    ]


def doubled(*arrays):
    return [a for a in arrays for _ in range(2)]


def paired(refs):
    return [refs[i : i + 2] for i in range(0, len(refs), 2)]


def planes_at(field, kx, ky, sea, t, half):
    land = strided(sea, (), t, half, ROWS).astype(jnp.float32)
    out = [strided(field, (l,), t, half, ROWS) * land for l in range(LEV)]
    return out + [land, strided(kx, (), t, half, ROWS), strided(ky, (), t, half, ROWS)]


def pack_kernel(links, *refs):
    field, kx, ky, sea = paired(refs[:8])
    west, east, north, nw, ne, rows = refs[8:]
    lane = lanes()
    group = lane // 16
    for t in range(ROWS):
        low = planes_at(field, kx, ky, sea, t, 0)
        high = planes_at(field, kx, ky, sea, t, 1)
        w, e = low[0], roll(high[0], 16)
        for p in range(1, PLANES):
            w = jnp.where(group == SLOT[p], roll(low[p], 16 * SLOT[p]), w)
            e = jnp.where(group == SLOT[p], roll(high[p], 16 * SLOT[p] + 16), e)
        west[8 * t : 8 * t + 8, :] = w
        east[8 * t : 8 * t + 8, :] = e
    flip = 127 - lane
    for p in range(PLANES):
        for o in range(2):
            for half in range(2):
                at = pl.ds(SIDE - 16 + 8 * o, 8)
                if p <= LEV:
                    x = sea[half][at, :].astype(jnp.float32)
                    x = field[half][p, at, :] * x if p < LEV else x
                else:
                    x = (kx, ky)[p - LEV - 1][half][at, :]
                x = jnp.take_along_axis(x, flip, axis=1)
                rows[p, 8 * o : 8 * o + 8, 128 * (1 - half) : 128 * (1 - half) + 128] = x
    for k in range(16):
        north[:, k, :] = rows[:, 15 - k, :]
    west_open = jnp.where(links[0, 0] >= 0, 1.0, 0.0).astype(jnp.float32)
    east_open = jnp.where(links[0, 1] >= 0, 1.0, 0.0).astype(jnp.float32)
    north[LEV, 14, :] = jnp.full((SIDE,), 1.0, jnp.float32) * west_open
    north[LEV, 15, :] = jnp.full((SIDE,), 1.0, jnp.float32) * east_open
    swap = jnp.bitwise_xor(lane, 15)
    for k in range(16):
        r = 8 * (ROWS - 1 - k) + 7
        nw[k : k + 1, :] = west[r : r + 1, :]
        ne[k : k + 1, :] = east[r : r + 1, :]
    for o in range(2):
        nw[8 * o : 8 * o + 8, :] = jnp.take_along_axis(nw[8 * o : 8 * o + 8, :], swap, axis=1)
        ne[8 * o : 8 * o + 8, :] = jnp.take_along_axis(ne[8 * o : 8 * o + 8, :], swap, axis=1)


def pack(links, field, kx, ky, sea):
    f32 = jnp.float32
    shapes = [(SIDE, 128), (SIDE, 128), (PLANES, 16, SIDE), (16, 128), (16, 128)]
    return pl.pallas_call(
        pack_kernel,
        out_shape=[jax.ShapeDtypeStruct(s, f32) for s in shapes],
        grid=(1,),
        in_specs=[SMEM] + half_specs((LEV,), (), (), ()),
        out_specs=[VMEM] * 5,
        scratch_shapes=[pltpu.VMEM((PLANES, 16, SIDE), f32)],
        compiler_params=pltpu.CompilerParams(vmem_limit_bytes=60 << 20),
        name="pack",
    )(links, *doubled(field, kx, ky, sea))


EVEN, ODD = slice(0, 128), slice(128, 256)
HALVES = (EVEN, ODD)


def sorter():
    col = lax.broadcasted_iota(jnp.int32, (SIDE, SIDE), 0)
    at = lax.broadcasted_iota(jnp.int32, (SIDE, SIDE), 1)
    want = jnp.where(at < 128, 2 * at, 2 * at - 255)
    return (col == want).astype(jnp.float32).astype(jnp.bfloat16)


def sort_columns(x, right):
    big = x.astype(jnp.bfloat16)
    small = (x - big.astype(jnp.float32)).astype(jnp.bfloat16)
    return jnp.dot(big, right, preferred_element_type=jnp.float32) + jnp.dot(
        small, right, preferred_element_type=jnp.float32
    )


def wide_weights(sea, kx, ky, rows, we, ww, wn):
    lane, sub = lanes(), sublanes()
    for t in range(rows):
        s = [sea(t, h) for h in range(2)]
        x = [kx(t, h) for h in range(2)]
        we[t, :, EVEN] = 0.5 * (x[0] + x[1]) * s[0] * s[1]
        w = 0.5 * (x[1] + roll(x[0], -1)) * s[1] * roll(s[0], -1)
        w = jnp.where(lane == 127, 0.0, w)
        we[t, :, ODD] = w
        ww[t] = roll(w, 1)
        for h in range(2):
            if t < rows - 1:
                sn, yn = sea(t + 1, h), ky(t + 1, h)
            else:
                sn, yn = up(sea(0, h)), up(ky(0, h))
            w = 0.5 * (ky(t, h) + yn) * s[h] * sn
            if t == rows - 1:
                w = jnp.where(sub == 7, 0.0, w)
            wn[t, :, HALVES[h]] = w


def wide_step(src, dst, we, ww, wn, rows, levels):
    below = []
    for l in levels:
        for h in HALVES:
            over = up(src[l, 0, :, h])
            src[l, rows, :, h] = over
            below.append(down(wn[rows - 1, :, h] * (over - src[l, rows - 1, :, h])))
    here = [src[l, 0, :, h] for l in levels for h in HALVES]
    for t in range(rows):
        e = [we[t, :, h] for h in HALVES]
        n = [wn[t, :, h] for h in HALVES]
        w = ww[t]
        nxt = [src[l, t + 1, :, h] for l in levels for h in HALVES]
        flux = [n[i % 2] * (nxt[i] - here[i]) for i in range(len(here))]
        for i, l in zip(range(0, len(here), 2), levels):
            a, b = here[i : i + 2]
            f = e[0] * (b - a)
            dst[l, t, :, EVEN] = (a + f) + w * (roll(b, 1) - a) + (flux[i] - below[i])
            dst[l, t, :, ODD] = (b - f) + e[1] * (roll(a, -1) - b) + (flux[i + 1] - below[i + 1])
        here, below = nxt, flux


def mixing(vertical):
    levels = vertical.shape[0]
    size = 16 * levels

    def at(shape, axis):
        return lax.broadcasted_iota(jnp.int32, shape, axis)

    left = (at((size, levels), 0) // 16 == at((size, levels), 1)).astype(jnp.float32).astype(jnp.bfloat16)
    right = (at((levels, size), 1) // 16 == at((levels, size), 0)).astype(jnp.float32).astype(jnp.bfloat16)
    tall = jnp.dot(left, vertical, preferred_element_type=jnp.float32).astype(jnp.bfloat16)
    full = jnp.dot(tall, right, preferred_element_type=jnp.float32)
    same = at((size, size), 0) % 16 == at((size, size), 1) % 16
    return jnp.where(same, full, 0.0).astype(jnp.bfloat16)


def own_tile(low, high, i):
    group = lanes() // 32
    a, b = TILES[i]
    x = jnp.where(group == 0, roll(low[a], HALO), roll(high[a], 32 - 108))
    y = jnp.where(group == 2, roll(low[b], 64 + HALO), roll(high[b], 96 - 108))
    return jnp.where(group < 2, x, y)


def inner_kernel(*refs):
    field, kx, ky, sea = paired(refs[:8])
    vertical, cur, own, top, mixer, other, raw, st, we, ww, wn = refs[8:]
    for t in range(ROWS):
        low = planes_at(field, kx, ky, sea, t, 0)
        high = planes_at(field, kx, ky, sea, t, 1)
        for p in range(PLANES):
            raw[p, t, :, 0:128] = low[p]
            raw[p, t, :, 128:256] = high[p]
        for i in range(4):
            own[i, t] = own_tile(low, high, i)
    right = sorter()
    for p in range(PLANES):
        x = sort_columns(raw[p].reshape(SIDE, SIDE), right).reshape(ROWS, 8, SIDE)
        if p < LEV:
            cur[p, 0:ROWS] = x
        else:
            st[p - LEV] = x

    def plane(p):
        return lambda t, h: st[p, t, :, HALVES[h]]

    wide_weights(plane(0), plane(1), plane(2), ROWS, we, ww, wn)
    for h in range(2):
        cols = slice(128 * h, 128 * h + 128)
        land = sea[h][SIDE - TOP :, :].astype(jnp.float32)
        for l in range(LEV):
            top[l, :, cols] = field[h][l, SIDE - TOP :, :] * land
        top[LEV, :, cols] = land
        top[LEV + 1, :, cols] = kx[h][SIDE - TOP :, :]
        top[LEV + 2, :, cols] = ky[h][SIDE - TOP :, :]
    mixer[...] = mixing(vertical[...])

    def two_steps(_, none):
        wide_step(cur, other, we, ww, wn, ROWS, range(LEV))
        wide_step(other, cur, we, ww, wn, ROWS, range(LEV))
        return none

    lax.fori_loop(0, STEPS // 2, two_steps, 0)


def inner(field, kx, ky, sea, vertical):
    f32 = jnp.float32
    scratch = [
        (LEV, ROWS + 1, 8, SIDE),
        (PLANES, ROWS, 8, SIDE),
        (3, ROWS, 8, SIDE),
        (ROWS, 8, SIDE),
        (ROWS, 8, 128),
        (ROWS, 8, SIDE),
    ]
    shapes = [(LEV, ROWS + 1, 8, SIDE), (4, ROWS, 8, 128), (PLANES, TOP, SIDE)]
    return pl.pallas_call(
        inner_kernel,
        out_shape=[jax.ShapeDtypeStruct(s, f32) for s in shapes] + [jax.ShapeDtypeStruct((640, 640), jnp.bfloat16)],
        grid=(1,),
        in_specs=half_specs((LEV,), (), (), ()) + [VMEM],
        out_specs=[VMEM] * 4,
        scratch_shapes=[pltpu.VMEM(s, f32) for s in scratch],
        compiler_params=pltpu.CompilerParams(vmem_limit_bytes=24 << 20),
        cost_estimate=pl.CostEstimate(flops=40_000_000, bytes_accessed=40_000_000, transcendentals=0),
        name="inner",
    )(*doubled(field, kx, ky, sea), vertical)


def strip_step(src, dst, we, ww, wn, tiles):
    sub = sublanes()
    below = []
    for k in tiles:
        over = jnp.where(sub == 7, src[k, ROWS], up(src[k, 0]))
        src[k, ROWS] = over
        below.append(jnp.where(sub == 0, 0.0, down(wn[ROWS - 1] * (over - src[k, ROWS - 1]))))
    here = [src[k, 0] for k in tiles]
    for t in range(STRIP):
        e, w, n = we[t], ww[t], wn[t]
        nxt = [src[k, t + 1] for k in tiles]
        flux = [n * (x - c) for x, c in zip(nxt, here)]
        for k, c, f, g in zip(tiles, here, flux, below):
            dst[k, t] = c + e * (roll(c, -1) - c) + w * (roll(c, 1) - c) + (f - g)
        here, below = nxt, flux


def rim_kernel(links, inside, own, top, west, east, north, nw, ne, out, cur, other, we, ww, wn, kap, sea, ext, nbr, nb_even, nb_odd, nc, n_other, nwe, nww, nwn):
    lane, sub = lanes(), sublanes()
    group, part = lane // 32, lane % 32
    w_halo = (part < HALO) & (group % 2 == 0)
    e_halo = (part >= 20) & (group % 2 == 1)
    ones = jnp.ones((8, 128), jnp.float32)

    def with_halo(i, mine, w, e):
        x = jnp.where(w_halo, roll(w, W_SHIFT[i]), mine)
        return jnp.where(e_halo, roll(e, E_SHIFT[i]), x)

    strips = (cur.at[0], cur.at[1], cur.at[2], kap)
    for t in range(ROWS):
        w, e = west[8 * t : 8 * t + 8, :], east[8 * t : 8 * t + 8, :]
        for i in range(4):
            strips[i][t] = with_halo(i, own[i, t], w, e)
    for o in range(2):
        rows = slice(8 * o, 8 * o + 8)
        low = [north[p, rows, 0:128] for p in range(PLANES)]
        high = [north[p, rows, 128:256] for p in range(PLANES)]
        for i in range(4):
            ext[i, rows, :] = with_halo(i, own_tile(low, high, i), nw[rows, :], ne[rows, :])
    for k in range(DEPTH):
        for i in range(4):
            strips[i][ROWS + k] = jnp.broadcast_to(ext[i, k : k + 1, :], (8, 128))

    def flag(x):
        return jnp.where(x >= 0, 1.0, 0.0).astype(jnp.float32)

    w_open = ones * flag(links[0, 0])
    e_open = ones * flag(links[0, 1])
    w_over = jnp.broadcast_to(north[LEV, 15:16, 0:128], (8, 128))
    e_over = jnp.broadcast_to(north[LEV, 14:15, 0:128], (8, 128))
    seams = []
    for a, b in ((w_open, e_open), (w_over, e_over)):
        m = jnp.where(lane == HALO - 1, a, jnp.where(lane == 32 + 19, b, 1.0))
        seams.append(0.5 * jnp.where(part == 31, 0.0, m))
    first = group < 2
    for t in range(STRIP):
        c = cur[2, t]
        sea[t] = jnp.where(first, roll(c, 64), c)
    for t in range(STRIP):
        s, x = sea[t], kap[t]
        w = seams[t >= ROWS] * (x + roll(x, -1)) * s * roll(s, -1)
        w = jnp.where(first, w, roll(w, 64))
        we[t] = w
        ww[t] = roll(w, 1)
        if t < STRIP - 1:
            sn, yn = sea[t + 1], kap[t + 1]
            if t == ROWS - 1:
                sn = jnp.where(sub == 7, sn, up(sea[0]))
                yn = jnp.where(sub == 7, yn, up(kap[0]))
            w = 0.5 * (x + yn) * s * sn
            wn[t] = jnp.where(first, roll(w, 64), w)
    zeros = jnp.zeros((8, 128), jnp.float32)
    wn[STRIP - 1] = zeros
    for i in range(3):
        cur[i, STRIP] = zeros
        other[i, STRIP] = zeros

    nbr[:, 0:TOP, :] = top[...]
    nbr[:, TOP : TOP + 16, :] = north[...]
    x = sort_columns(nbr[...].reshape(PLANES * (TOP + 16), SIDE), sorter()).reshape(PLANES, TOP + 16, SIDE)
    nb = (nb_even, nb_odd)
    for h in range(2):
        nb[h][...] = x[:, :, HALVES[h]]
    for l in range(LEV):
        for t in range(NORTH):
            for h in range(2):
                nc[l, t, :, HALVES[h]] = strided(nb, (l,), t, h, NORTH)

    def plane(p):
        return lambda t, h: strided(nb, (p,), t, h, NORTH)

    wide_weights(plane(LEV), plane(LEV + 1), plane(LEV + 2), NORTH, nwe, nww, nwn)

    def two_steps(_, none):
        strip_step(cur, other, we, ww, wn, range(3))
        wide_step(nc, n_other, nwe, nww, nwn, NORTH, range(LEV))
        strip_step(other, cur, we, ww, wn, range(3))
        wide_step(n_other, nc, nwe, nww, nwn, NORTH, range(LEV))
        return none

    lax.fori_loop(0, STEPS // 2, two_steps, 0)

    for l in range(LEV):
        for t in range(NORTH):
            for h in range(2):
                nb[h][l, pl.ds(t, 8, stride=NORTH), :] = nc[l, t, :, HALVES[h]]

    on_rim = (lane < 5) | (lane >= 123)
    top_row = sub == 7
    for l in range(LEV):
        i, base = l // 2, 64 * (l % 2)
        pick = [
            jnp.where(lane < 5, base + HALO + 2 * lane + h, jnp.where(lane >= 123, base + 42 + 2 * (lane - 123) + h, 0))
            for h in range(2)
        ]
        for t in range(0, ROWS, 2):
            pair = []
            for u in (t, t + 1):
                for h in range(2):
                    x = inside[l, u, :, HALVES[h]]
                    if u >= ROWS - DEPTH:
                        r = TOP - ROWS + u
                        x = jnp.where(top_row, jnp.broadcast_to(nb[h][l, r : r + 1, :], (8, 128)), x)
                    pair.append(jnp.where(on_rim, jnp.take_along_axis(cur[i, u], pick[h], axis=1), x))
            q, r = t // 4, 8 * (t % 4)
            for h in range(2):
                x = jnp.concatenate([pair[h], pair[2 + h]], axis=0)
                out[q, l, r : r + 16, HALVES[h]] = x.astype(jnp.bfloat16)


def rim(links, inside, own, top, west, east, north, nw, ne):
    f32 = jnp.float32
    scratch = [
        (3, STRIP + 1, 8, 128),
        (3, STRIP + 1, 8, 128),
        (STRIP, 8, 128),
        (STRIP, 8, 128),
        (STRIP, 8, 128),
        (STRIP, 8, 128),
        (STRIP, 8, 128),
        (4, 16, 128),
        (PLANES, TOP + 16, SIDE),
        (PLANES, TOP + 16, 128),
        (PLANES, TOP + 16, 128),
        (LEV, NORTH + 1, 8, SIDE),
        (LEV, NORTH + 1, 8, SIDE),
        (NORTH, 8, SIDE),
        (NORTH, 8, 128),
        (NORTH, 8, SIDE),
    ]
    return pl.pallas_call(
        rim_kernel,
        out_shape=jax.ShapeDtypeStruct((CHUNKS, LEV, SIDE // CHUNKS, SIDE), jnp.bfloat16),
        in_specs=[SMEM] + [VMEM] * 8,
        out_specs=VMEM,
        scratch_shapes=[pltpu.VMEM(s, f32) for s in scratch],
        compiler_params=pltpu.CompilerParams(vmem_limit_bytes=24 << 20),
        name="rim",
    )(links, inside, own, top, west, east, north, nw, ne)


def mix_kernel(x, k, y):
    for h in range(2):
        rows = x[:, :, 16 * h : 16 * h + 16, :].reshape(CHUNKS * LEV * 16, SIDE)
        mixed = jnp.dot(k[...], rows, preferred_element_type=jnp.float32).astype(jnp.bfloat16)
        y[:, :, 16 * h : 16 * h + 16, :] = mixed.reshape(CHUNKS, LEV, 16, SIDE)


def mix(x, k):
    return pl.pallas_call(
        mix_kernel,
        out_shape=jax.ShapeDtypeStruct(x.shape, jnp.bfloat16),
        in_specs=[VMEM] * 2,
        out_specs=VMEM,
        compiler_params=pltpu.CompilerParams(vmem_limit_bytes=24 << 20),
        name="mix",
    )(x, k)


def unpack_kernel(z, out):
    at = lax.broadcasted_iota(jnp.int32, (SIDE, 128), 0)
    col = lax.broadcasted_iota(jnp.int32, (SIDE, 128), 1) + 128 * pl.program_id(0)
    back = (jnp.where(at < 128, 2 * at, 2 * at - 255) == col).astype(jnp.float32).astype(jnp.bfloat16)
    for q in range(CHUNKS):
        x = jnp.dot(z[q].reshape(LEV * 32, SIDE), back, preferred_element_type=jnp.float32)
        for l in range(LEV):
            for u in range(4):
                r = 32 * l + 8 * u
                out[l, pl.ds(4 * q + u, 8, stride=ROWS), :] = x[r : r + 8]


def unpack(z):
    return pl.pallas_call(
        unpack_kernel,
        out_shape=jax.ShapeDtypeStruct((LEV, SIDE, SIDE), jnp.float32),
        grid=(2,),
        in_specs=[pl.BlockSpec((CHUNKS, LEV, SIDE // CHUNKS, SIDE), lambda h: (0, 0, 0, 0))],
        out_specs=pl.BlockSpec((LEV, SIDE, 128), lambda h: (0, 0, h)),
        compiler_params=pltpu.CompilerParams(vmem_limit_bytes=24 << 20),
        name="unpack",
    )(z)


def shards(field, kappa_x, kappa_y, sea_mask, tile_links, vertical):
    tiles = lax.axis_size("tile")

    def send(x, target):
        return lax.ppermute(x, "tile", [(i, target(i) % tiles) for i in range(tiles)])

    cells, kx, ky, sea = field[0], kappa_x[0], kappa_y[0], sea_mask[0]
    west, east, north, nw, ne = pack(tile_links, cells, kx, ky, sea)
    from_east = send(west, lambda i: i - 1)
    from_west = send(east, lambda i: i + 1)
    from_north = send(north, lambda i: -i)
    from_nw = send(nw, lambda i: 1 - i)
    from_ne = send(ne, lambda i: -1 - i)
    inside, own, top, mixer = inner(cells, kx, ky, sea, vertical)
    smooth = rim(tile_links, inside, own, top, from_west, from_east, from_north, from_nw, from_ne)
    gathered = lax.all_to_all(smooth, "lev", 0, 0, tiled=True)
    back = lax.all_to_all(mix(gathered, mixer), "lev", 0, 0, tiled=True)
    return unpack(back)[None]


def solution(mesh):
    placed = (
        P("tile", "lev", None, None),
        P("tile", None, None),
        P("tile", None, None),
        P("tile", None, None),
        P("tile", None),
        P(),
    )
    return jax.shard_map(
        shards, mesh=mesh, in_specs=placed, out_specs=P("tile", "lev", None, None), check_vma=False
    )
```

time: 100 us -> 84.3 us (0.84)
  Pallas kernels: 38.3 us -> 22.4 us
    pallas_call x1, Pallas kernels: 18.5 us -> 8.71 us  [rim(): pl.pallas_call(rim_kernel, out_shape=jax.ShapeDtypeStruct((CHUNKS, LEV, S...]
    pallas_call x1, Pallas kernels: 13.5 us -> 7.15 us  [inner(): pl.pallas_call(inner_kernel, out_shape=[jax.ShapeDtypeStruct(s, f32) for...]
  transfers between devices with their start and end apart: 5 -> 5, of which waited for: 0 -> 0; matrix products, arithmetic and copies ran while one was open for 0% -> 0% of each run, Pallas kernels for 13% -> 8%
where the time goes in v2:
time: 84.3 us; the launch traced here: 84.1 us
  blocking collectives  51.9 us (62%)
  Pallas kernels  22.4 us (27%)
  starting transfers between devices  9.65 us (11%)
    all_to_all x1, blocking collectives, shards(): gathered = lax.all_to_all(smooth, 'lev', 0, 0, tiled=True)  28.8 us
    all_to_all x1, blocking collectives, shards(): back = lax.all_to_all(mix(gathered, mixer), 'lev', 0, 0, tiled=True)  23.2 us
    ppermute x5, starting transfers between devices, send(): lax.ppermute(x, 'tile', [(i, target(i) % tiles) for i in range(tiles)])  9.65 us
    pallas_call x1, Pallas kernels, rim(): pl.pallas_call(rim_kernel, out_shape=jax.ShapeDtypeStruct((CHUNKS, LEV, S...  8.71 us
    pallas_call x1, Pallas kernels, inner(): pl.pallas_call(inner_kernel, out_shape=[jax.ShapeDtypeStruct(s, f32) for...  7.15 us
    pallas_call x1, Pallas kernels, pack(): pl.pallas_call(pack_kernel, out_shape=[jax.ShapeDtypeStruct(s, f32) for s...  3.89 us
    pallas_call x1, Pallas kernels, unpack(): pl.pallas_call(unpack_kernel, out_shape=jax.ShapeDtypeStruct((LEV, SIDE,...  1.99 us
  transfers between devices with their start and end apart: 5, of which 0 were waited for; matrix products, arithmetic and copies ran while one was open for 0% of the time, Pallas kernels for 8%

profile of v2, /device:TPU:15, one launch (start us, length us, event | category | flops | bytes accessed | tf_op | source)
XLA Modules:
  0.0 84.1 jit_solution(16386374477419423529)
XLA Ops:
  0.0 0.0 copy-start
  0.0 0.0 copy-start.1
  0.0 0.0 copy-start.2
  0.0 0.0 copy-start.3
  0.0 0.0 copy-start.4
  0.0 3.9 %pack.1 = (f32[256,128]{1,0:T(8,128)}, f32[256,128]{1,0:T(8,128)}, f32[8,16,256]{2,1,0:T(8,128)}, f32[16,128]{1,0:T(8,128)}, f32[16,128]{1,0:T(8,128)}) custom-call(s32[1,4]{1,0:T(1,128)} %links.3, f32[5,256,256]{2,1,0:T(8,128)} %bitcast.5, f32[5,256,256]{2,1,0:T(8,128)} %bitcast.6, f32[256,256]{1,0:T(8,128)} %bitcast.9, f32[256,256]{1,0:T(8,128)} %bitcast.10, ...), custom_call_target="tpu_custom_call" | custom-call | tf_op jit(solution)/shard_map/pack/pallas_call | solution.py:120
  3.9 1.9 %collective-permute-start = (f32[256,128]{1,0:T(8,128)}, f32[256,128]{1,0:T(8,128)S(1)}, u32[]{:S(2)}, u32[]{:S(2)}) collective-permute-start(f32[256,128]{1,0:T(8,128)} %get-tuple-element.17), channel_id=1, source_target_pairs={{0,8},{8,16},{16,24},{24,32},{32,40},{40,48},{48,56},{56,64},{64,7... | collective-permute-start | bytes 393224 | tf_op jit(solution)/shard_map/ppermute | solution.py:489
  5.8 0.0 collective-permute-start.1
  5.8 2.8 %collective-permute-start.2 = (f32[8,16,256]{2,1,0:T(8,128)}, f32[8,16,256]{2,1,0:T(8,128)S(1)}, u32[]{:S(2)}, u32[]{:S(2)}) collective-permute-start(f32[8,16,256]{2,1,0:T(8,128)} %get-tuple-element.19), channel_id=1, source_target_pairs={{0,0},{8,248},{16,240},{24,232},{32,224},{40,216},{48,208},{56,200... | collective-permute-start | bytes 393224 | tf_op jit(solution)/shard_map/ppermute | solution.py:489
  8.6 5.0 %collective-permute-start.3 = (f32[16,128]{1,0:T(8,128)}, f32[16,128]{1,0:T(8,128)S(1)}, u32[]{:S(2)}, u32[]{:S(2)}) collective-permute-start(f32[16,128]{1,0:T(8,128)} %get-tuple-element.20), channel_id=1, source_target_pairs={{0,8},{8,0},{16,248},{24,240},{32,232},{40,224},{48,216},{56,208},... | collective-permute-start | bytes 24584 | tf_op jit(solution)/shard_map/ppermute | solution.py:489
  13.6 0.0 copy-start.5
  13.6 0.0 collective-permute-start.4
  13.6 0.0 copy-done
  13.6 0.0 copy-done.1
  13.6 0.0 copy-done.2
  13.6 0.0 copy-done.3
  13.6 0.0 copy-done.4
  13.6 7.1 %inner.1 = (f32[5,33,8,256]{3,2,1,0:T(8,128)S(1)}, f32[4,32,8,128]{3,2,1,0:T(8,128)S(1)}, f32[8,24,256]{2,1,0:T(8,128)S(1)}, bf16[640,640]{1,0:T(8,128)(2,1)S(1)}) custom-call(f32[5,256,256]{2,1,0:T(8,128)S(1)} %bitcast.7, f32[5,256,256]{2,1,0:T(8,128)S(1)} %bitcast.8, f32[256,256]{1,0:T(8,128)S(1)} %bitcast.11, f32[256,256]{1,0:T(8,128)S(1)} %bitcast.12, ...), custom_call_target="tpu_custom_call" | custom-call | flops 40000000 | bytes 40000000 | tf_op jit(solution)/shard_map/inner/pallas_call | solution.py:269
  20.8 0.0 collective-permute-done.3.nw
  20.8 0.0 collective-permute-done.4.ne
  20.8 0.0 collective-permute-done.west
  20.8 0.0 collective-permute-done.1.east
  20.8 0.0 collective-permute-done.2.north
  20.8 0.0 copy-done.5
  20.8 8.7 %rim.1 = bf16[8,5,32,256]{3,2,1,0:T(8,128)(2,1)S(1)} custom-call(s32[1,4]{1,0:T(1,128)S(1)} %copy-done.5, f32[5,33,8,256]{3,2,1,0:T(8,128)S(1)} %get-tuple-element.14.inside, f32[4,32,8,128]{3,2,1,0:T(8,128)S(1)} %get-tuple-element.15.own, f32[8,24,256]{2,1,0:T(8,128)S(1)} %get-tuple-element.16.top, f32[256,128]{1,0:T(8,128)S(1)} %collective-permute-done.west, ...), custom_call_target="tpu_custom_call" | custom-call | tf_op jit(solution)/shard_map/rim/pallas_call | solution.py:432
  29.6 28.8 %all_to_all.10.x = bf16[8,5,32,256]{3,2,1,0:T(8,128)(2,1)S(1)} all-to-all(bf16[8,5,32,256]{3,2,1,0:T(8,128)(2,1)S(1)} %rim.1), channel_id=1, replica_groups=mesh['tile'=32,'lev'=8] {'lev'}, dimensions={0} | all-to-all | bytes 1310720 | tf_op jit(solution)/shard_map/all_to_all | solution.py:500
  58.3 0.7 mix.1
  59.0 23.2 %all_to_all.11.z = bf16[8,5,32,256]{3,2,1,0:T(8,128)(2,1)S(1)} all-to-all(bf16[8,5,32,256]{3,2,1,0:T(8,128)(2,1)S(1)} %mix.1), channel_id=1, replica_groups=mesh['tile'=32,'lev'=8] {'lev'}, dimensions={0} | all-to-all | bytes 1310720 | tf_op jit(solution)/shard_map/all_to_all | solution.py:501
  82.2 2.0 %unpack.1 = f32[5,256,256]{2,1,0:T(8,128)} custom-call(bf16[8,5,32,256]{3,2,1,0:T(8,128)(2,1)S(1)} %all_to_all.11.z), custom_call_target="tpu_custom_call" | custom-call | tf_op jit(solution)/shard_map/unpack/pallas_call | solution.py:474
Async XLA Ops:
  0.0 13.6 %copy-start = (f32[1,5,256,256]{3,2,1,0:T(8,128)S(1)}, f32[1,5,256,256]{3,2,1,0:T(8,128)}, u32[]{:S(2)}) copy-start(f32[1,5,256,256]{3,2,1,0:T(8,128)} %param.6) | copy-start | bytes 3932164
  0.0 13.6 %copy-start.1 = (f32[1,256,256]{2,1,0:T(8,128)S(1)}, f32[1,256,256]{2,1,0:T(8,128)}, u32[]{:S(2)}) copy-start(f32[1,256,256]{2,1,0:T(8,128)} %param.7) | copy-start | bytes 786436
  0.0 13.6 %copy-start.2 = (f32[1,256,256]{2,1,0:T(8,128)S(1)}, f32[1,256,256]{2,1,0:T(8,128)}, u32[]{:S(2)}) copy-start(f32[1,256,256]{2,1,0:T(8,128)} %param.8) | copy-start | bytes 786436
  0.0 13.6 %copy-start.3 = (s32[1,256,256]{2,1,0:T(8,128)S(1)}, s32[1,256,256]{2,1,0:T(8,128)}, u32[]{:S(2)}) copy-start(s32[1,256,256]{2,1,0:T(8,128)} %param.9) | copy-start | bytes 786436
  0.0 13.6 %copy-start.4 = (bf16[40,40]{1,0:T(8,128)(2,1)S(1)}, bf16[40,40]{1,0:T(8,128)(2,1)}, u32[]{:S(2)}) copy-start(bf16[40,40]{1,0:T(8,128)(2,1)} %refs_8_.1) | copy-start | bytes 9604
  3.9 16.9 %collective-permute-start = (f32[256,128]{1,0:T(8,128)}, f32[256,128]{1,0:T(8,128)S(1)}, u32[]{:S(2)}, u32[]{:S(2)}) collective-permute-start(f32[256,128]{1,0:T(8,128)} %get-tuple-element.17), channel_id=1, source_target_pairs={{0,8},{8,16},{16,24},{24,32},{32,40},{40,48},{48,56},{56,64},{64,7... | collective-permute-start | bytes 393224 | tf_op jit(solution)/shard_map/ppermute | solution.py:489
  5.8 15.0 %collective-permute-start.1 = (f32[256,128]{1,0:T(8,128)}, f32[256,128]{1,0:T(8,128)S(1)}, u32[]{:S(2)}, u32[]{:S(2)}) collective-permute-start(f32[256,128]{1,0:T(8,128)} %get-tuple-element.18), channel_id=1, source_target_pairs={{0,248},{8,0},{16,8},{24,16},{32,24},{40,32},{48,40},{56,48},{64,5... | collective-permute-start | bytes 393224 | tf_op jit(solution)/shard_map/ppermute | solution.py:489
  5.8 15.0 %collective-permute-start.2 = (f32[8,16,256]{2,1,0:T(8,128)}, f32[8,16,256]{2,1,0:T(8,128)S(1)}, u32[]{:S(2)}, u32[]{:S(2)}) collective-permute-start(f32[8,16,256]{2,1,0:T(8,128)} %get-tuple-element.19), channel_id=1, source_target_pairs={{0,0},{8,248},{16,240},{24,232},{32,224},{40,216},{48,208},{56,200... | collective-permute-start | bytes 393224 | tf_op jit(solution)/shard_map/ppermute | solution.py:489
  8.6 12.2 %collective-permute-start.3 = (f32[16,128]{1,0:T(8,128)}, f32[16,128]{1,0:T(8,128)S(1)}, u32[]{:S(2)}, u32[]{:S(2)}) collective-permute-start(f32[16,128]{1,0:T(8,128)} %get-tuple-element.20), channel_id=1, source_target_pairs={{0,8},{8,0},{16,248},{24,240},{32,232},{40,224},{48,216},{56,208},... | collective-permute-start | bytes 24584 | tf_op jit(solution)/shard_map/ppermute | solution.py:489
  13.6 7.3 %copy-start.5 = (s32[1,4]{1,0:T(1,128)S(1)}, s32[1,4]{1,0:T(1,128)}, u32[]{:S(2)}) copy-start(s32[1,4]{1,0:T(1,128)} %links.3) | copy-start | bytes 52
  13.6 7.2 %collective-permute-start.4 = (f32[16,128]{1,0:T(8,128)}, f32[16,128]{1,0:T(8,128)S(1)}, u32[]{:S(2)}, u32[]{:S(2)}) collective-permute-start(f32[16,128]{1,0:T(8,128)} %get-tuple-element.21), channel_id=1, source_target_pairs={{0,248},{8,240},{16,232},{24,224},{32,216},{40,208},{48,200},{56,1... | collective-permute-start | bytes 24584 | tf_op jit(solution)/shard_map/ppermute | solution.py:489

commit v3 on v2

--- a/solution.py
+++ b/solution.py
@@ -308,10 +308,16 @@
         return jnp.where(e_halo, roll(e, E_SHIFT[i]), x)
 
     strips = (cur.at[0], cur.at[1], cur.at[2], kap)
-    for t in range(ROWS):
-        w, e = west[8 * t : 8 * t + 8, :], east[8 * t : 8 * t + 8, :]
-        for i in range(4):
-            strips[i][t] = with_halo(i, own[i, t], w, e)
+    def fill(b, none):
+        for j in range(8):
+            t = 8 * b + j
+            at = pl.ds(pl.multiple_of(8 * t, 8), 8)
+            w, e = west[at, :], east[at, :]
+            for i in range(4):
+                strips[i][t] = with_halo(i, own[i, t], w, e)
+        return none
+
+    lax.fori_loop(0, ROWS // 8, fill, 0)
     for o in range(2):
         rows = slice(8 * o, 8 * o + 8)
         low = [north[p, rows, 0:128] for p in range(PLANES)]
@@ -334,22 +340,36 @@
         m = jnp.where(lane == HALO - 1, a, jnp.where(lane == 32 + 19, b, 1.0))
         seams.append(0.5 * jnp.where(part == 31, 0.0, m))
     first = group < 2
-    for t in range(STRIP):
-        c = cur[2, t]
-        sea[t] = jnp.where(first, roll(c, 64), c)
-    for t in range(STRIP):
-        s, x = sea[t], kap[t]
-        w = seams[t >= ROWS] * (x + roll(x, -1)) * s * roll(s, -1)
+    def spread_sea(b, none):
+        for j in range(14):
+            c = cur[2, 14 * b + j]
+            sea[14 * b + j] = jnp.where(first, roll(c, 64), c)
+        return none
+
+    lax.fori_loop(0, STRIP // 14, spread_sea, 0)
+
+    def weights(t, seam, s, x, sn, yn):
+        w = seam * (x + roll(x, -1)) * s * roll(s, -1)
         w = jnp.where(first, w, roll(w, 64))
         we[t] = w
         ww[t] = roll(w, 1)
-        if t < STRIP - 1:
-            sn, yn = sea[t + 1], kap[t + 1]
-            if t == ROWS - 1:
-                sn = jnp.where(sub == 7, sn, up(sea[0]))
-                yn = jnp.where(sub == 7, yn, up(kap[0]))
-            w = 0.5 * (x + yn) * s * sn
-            wn[t] = jnp.where(first, roll(w, 64), w)
+        w = 0.5 * (x + yn) * s * sn
+        wn[t] = jnp.where(first, roll(w, 64), w)
+
+    def most_weights(b, none):
+        for j in range(14):
+            t = 14 * b + j
+            weights(t, seams[0], sea[t], kap[t], sea[t + 1], kap[t + 1])
+        return none
+
+    lax.fori_loop(0, 2, most_weights, 0)
+    for t in range(28, STRIP):
+        s, x = sea[t], kap[t]
+        sn, yn = (sea[t + 1], kap[t + 1]) if t < STRIP - 1 else (s, x)
+        if t == ROWS - 1:
+            sn = jnp.where(sub == 7, sn, up(sea[0]))
+            yn = jnp.where(sub == 7, yn, up(kap[0]))
+        weights(t, seams[t >= ROWS], s, x, sn, yn)
     zeros = jnp.zeros((8, 128), jnp.float32)
     wn[STRIP - 1] = zeros
     for i in range(3):

time: 84.3 us -> 82 us (0.973)
  Pallas kernels: 22.4 us -> 20.1 us
    pallas_call x1, Pallas kernels: 8.71 us -> 6.39 us  [rim(): pl.pallas_call(rim_kernel, out_shape=jax.ShapeDtypeStruct((CHUNKS, LEV, S...]
  transfers between devices with their start and end apart: 5 -> 5, of which waited for: 0 -> 0; matrix products, arithmetic and copies ran while one was open for 0% -> 0% of each run, Pallas kernels for 8% -> 9%
where the time goes in v3:
time: 82 us; the launch traced here: 81.8 us
  blocking collectives  51.9 us (63%)
  Pallas kernels  20.1 us (25%)
  starting transfers between devices  9.65 us (12%)
    all_to_all x1, blocking collectives, shards(): gathered = lax.all_to_all(smooth, 'lev', 0, 0, tiled=True)  28.8 us
    all_to_all x1, blocking collectives, shards(): back = lax.all_to_all(mix(gathered, mixer), 'lev', 0, 0, tiled=True)  23.1 us
    ppermute x5, starting transfers between devices, send(): lax.ppermute(x, 'tile', [(i, target(i) % tiles) for i in range(tiles)])  9.65 us
    pallas_call x1, Pallas kernels, inner(): pl.pallas_call(inner_kernel, out_shape=[jax.ShapeDtypeStruct(s, f32) for...  7.15 us
    pallas_call x1, Pallas kernels, rim(): pl.pallas_call(rim_kernel, out_shape=jax.ShapeDtypeStruct((CHUNKS, LEV, S...  6.39 us
    pallas_call x1, Pallas kernels, pack(): pl.pallas_call(pack_kernel, out_shape=[jax.ShapeDtypeStruct(s, f32) for s...  3.89 us
    pallas_call x1, Pallas kernels, unpack(): pl.pallas_call(unpack_kernel, out_shape=jax.ShapeDtypeStruct((LEV, SIDE,...  1.99 us
  transfers between devices with their start and end apart: 5, of which 0 were waited for; matrix products, arithmetic and copies ran while one was open for 0% of the time, Pallas kernels for 9%

profile of v3, /device:TPU:15, one launch (start us, length us, event | category | flops | bytes accessed | tf_op | source)
XLA Modules:
  0.0 81.8 jit_solution(5040802744305973238)
XLA Ops:
  0.0 0.0 copy-start
  0.0 0.0 copy-start.1
  0.0 0.0 copy-start.2
  0.0 0.0 copy-start.3
  0.0 0.0 copy-start.4
  0.0 3.9 %pack.1 = (f32[256,128]{1,0:T(8,128)}, f32[256,128]{1,0:T(8,128)}, f32[8,16,256]{2,1,0:T(8,128)}, f32[16,128]{1,0:T(8,128)}, f32[16,128]{1,0:T(8,128)}) custom-call(s32[1,4]{1,0:T(1,128)} %links.3, f32[5,256,256]{2,1,0:T(8,128)} %bitcast.5, f32[5,256,256]{2,1,0:T(8,128)} %bitcast.6, f32[256,256]{1,0:T(8,128)} %bitcast.9, f32[256,256]{1,0:T(8,128)} %bitcast.10, ...), custom_call_target="tpu_custom_call" | custom-call | tf_op jit(solution)/shard_map/pack/pallas_call | solution.py:120
  3.9 1.9 %collective-permute-start = (f32[256,128]{1,0:T(8,128)}, f32[256,128]{1,0:T(8,128)S(1)}, u32[]{:S(2)}, u32[]{:S(2)}) collective-permute-start(f32[256,128]{1,0:T(8,128)} %get-tuple-element.17), channel_id=1, source_target_pairs={{0,8},{8,16},{16,24},{24,32},{32,40},{40,48},{48,56},{56,64},{64,7... | collective-permute-start | bytes 393224 | tf_op jit(solution)/shard_map/ppermute | solution.py:509
  5.8 0.0 collective-permute-start.1
  5.8 2.8 %collective-permute-start.2 = (f32[8,16,256]{2,1,0:T(8,128)}, f32[8,16,256]{2,1,0:T(8,128)S(1)}, u32[]{:S(2)}, u32[]{:S(2)}) collective-permute-start(f32[8,16,256]{2,1,0:T(8,128)} %get-tuple-element.19), channel_id=1, source_target_pairs={{0,0},{8,248},{16,240},{24,232},{32,224},{40,216},{48,208},{56,200... | collective-permute-start | bytes 393224 | tf_op jit(solution)/shard_map/ppermute | solution.py:509
  8.6 5.0 %collective-permute-start.3 = (f32[16,128]{1,0:T(8,128)}, f32[16,128]{1,0:T(8,128)S(1)}, u32[]{:S(2)}, u32[]{:S(2)}) collective-permute-start(f32[16,128]{1,0:T(8,128)} %get-tuple-element.20), channel_id=1, source_target_pairs={{0,8},{8,0},{16,248},{24,240},{32,232},{40,224},{48,216},{56,208},... | collective-permute-start | bytes 24584 | tf_op jit(solution)/shard_map/ppermute | solution.py:509
  13.6 0.0 copy-start.5
  13.6 0.0 collective-permute-start.4
  13.6 0.0 copy-done
  13.6 0.0 copy-done.1
  13.6 0.0 copy-done.2
  13.6 0.0 copy-done.3
  13.6 0.0 copy-done.4
  13.6 7.1 %inner.1 = (f32[5,33,8,256]{3,2,1,0:T(8,128)S(1)}, f32[4,32,8,128]{3,2,1,0:T(8,128)S(1)}, f32[8,24,256]{2,1,0:T(8,128)S(1)}, bf16[640,640]{1,0:T(8,128)(2,1)S(1)}) custom-call(f32[5,256,256]{2,1,0:T(8,128)S(1)} %bitcast.7, f32[5,256,256]{2,1,0:T(8,128)S(1)} %bitcast.8, f32[256,256]{1,0:T(8,128)S(1)} %bitcast.11, f32[256,256]{1,0:T(8,128)S(1)} %bitcast.12, ...), custom_call_target="tpu_custom_call" | custom-call | flops 40000000 | bytes 40000000 | tf_op jit(solution)/shard_map/inner/pallas_call | solution.py:269
  20.8 0.0 collective-permute-done.3.nw
  20.8 0.0 collective-permute-done.4.ne
  20.8 0.0 collective-permute-done.west
  20.8 0.0 collective-permute-done.1.east
  20.8 0.0 collective-permute-done.2.north
  20.8 0.0 copy-done.5
  20.8 6.4 %rim.1 = bf16[8,5,32,256]{3,2,1,0:T(8,128)(2,1)S(1)} custom-call(s32[1,4]{1,0:T(1,128)S(1)} %copy-done.5, f32[5,33,8,256]{3,2,1,0:T(8,128)S(1)} %get-tuple-element.14.inside, f32[4,32,8,128]{3,2,1,0:T(8,128)S(1)} %get-tuple-element.15.own, f32[8,24,256]{2,1,0:T(8,128)S(1)} %get-tuple-element.16.top, f32[256,128]{1,0:T(8,128)S(1)} %collective-permute-done.west, ...), custom_call_target="tpu_custom_call" | custom-call | tf_op jit(solution)/shard_map/rim/pallas_call | solution.py:452
  27.2 28.8 %all_to_all.10.x = bf16[8,5,32,256]{3,2,1,0:T(8,128)(2,1)S(1)} all-to-all(bf16[8,5,32,256]{3,2,1,0:T(8,128)(2,1)S(1)} %rim.1), channel_id=1, replica_groups=mesh['tile'=32,'lev'=8] {'lev'}, dimensions={0} | all-to-all | bytes 1310720 | tf_op jit(solution)/shard_map/all_to_all | solution.py:520
  56.0 0.7 mix.1
  56.7 23.1 %all_to_all.11.z = bf16[8,5,32,256]{3,2,1,0:T(8,128)(2,1)S(1)} all-to-all(bf16[8,5,32,256]{3,2,1,0:T(8,128)(2,1)S(1)} %mix.1), channel_id=1, replica_groups=mesh['tile'=32,'lev'=8] {'lev'}, dimensions={0} | all-to-all | bytes 1310720 | tf_op jit(solution)/shard_map/all_to_all | solution.py:521
  79.8 2.0 %unpack.1 = f32[5,256,256]{2,1,0:T(8,128)} custom-call(bf16[8,5,32,256]{3,2,1,0:T(8,128)(2,1)S(1)} %all_to_all.11.z), custom_call_target="tpu_custom_call" | custom-call | tf_op jit(solution)/shard_map/unpack/pallas_call | solution.py:494
Async XLA Ops:
  0.0 13.6 %copy-start = (f32[1,5,256,256]{3,2,1,0:T(8,128)S(1)}, f32[1,5,256,256]{3,2,1,0:T(8,128)}, u32[]{:S(2)}) copy-start(f32[1,5,256,256]{3,2,1,0:T(8,128)} %param.6) | copy-start | bytes 3932164
  0.0 13.6 %copy-start.1 = (f32[1,256,256]{2,1,0:T(8,128)S(1)}, f32[1,256,256]{2,1,0:T(8,128)}, u32[]{:S(2)}) copy-start(f32[1,256,256]{2,1,0:T(8,128)} %param.7) | copy-start | bytes 786436
  0.0 13.6 %copy-start.2 = (f32[1,256,256]{2,1,0:T(8,128)S(1)}, f32[1,256,256]{2,1,0:T(8,128)}, u32[]{:S(2)}) copy-start(f32[1,256,256]{2,1,0:T(8,128)} %param.8) | copy-start | bytes 786436
  0.0 13.6 %copy-start.3 = (s32[1,256,256]{2,1,0:T(8,128)S(1)}, s32[1,256,256]{2,1,0:T(8,128)}, u32[]{:S(2)}) copy-start(s32[1,256,256]{2,1,0:T(8,128)} %param.9) | copy-start | bytes 786436
  0.0 13.6 %copy-start.4 = (bf16[40,40]{1,0:T(8,128)(2,1)S(1)}, bf16[40,40]{1,0:T(8,128)(2,1)}, u32[]{:S(2)}) copy-start(bf16[40,40]{1,0:T(8,128)(2,1)} %refs_8_.1) | copy-start | bytes 9604
  3.9 16.9 %collective-permute-start = (f32[256,128]{1,0:T(8,128)}, f32[256,128]{1,0:T(8,128)S(1)}, u32[]{:S(2)}, u32[]{:S(2)}) collective-permute-start(f32[256,128]{1,0:T(8,128)} %get-tuple-element.17), channel_id=1, source_target_pairs={{0,8},{8,16},{16,24},{24,32},{32,40},{40,48},{48,56},{56,64},{64,7... | collective-permute-start | bytes 393224 | tf_op jit(solution)/shard_map/ppermute | solution.py:509
  5.8 15.0 %collective-permute-start.1 = (f32[256,128]{1,0:T(8,128)}, f32[256,128]{1,0:T(8,128)S(1)}, u32[]{:S(2)}, u32[]{:S(2)}) collective-permute-start(f32[256,128]{1,0:T(8,128)} %get-tuple-element.18), channel_id=1, source_target_pairs={{0,248},{8,0},{16,8},{24,16},{32,24},{40,32},{48,40},{56,48},{64,5... | collective-permute-start | bytes 393224 | tf_op jit(solution)/shard_map/ppermute | solution.py:509
  5.8 15.0 %collective-permute-start.2 = (f32[8,16,256]{2,1,0:T(8,128)}, f32[8,16,256]{2,1,0:T(8,128)S(1)}, u32[]{:S(2)}, u32[]{:S(2)}) collective-permute-start(f32[8,16,256]{2,1,0:T(8,128)} %get-tuple-element.19), channel_id=1, source_target_pairs={{0,0},{8,248},{16,240},{24,232},{32,224},{40,216},{48,208},{56,200... | collective-permute-start | bytes 393224 | tf_op jit(solution)/shard_map/ppermute | solution.py:509
  8.6 12.2 %collective-permute-start.3 = (f32[16,128]{1,0:T(8,128)}, f32[16,128]{1,0:T(8,128)S(1)}, u32[]{:S(2)}, u32[]{:S(2)}) collective-permute-start(f32[16,128]{1,0:T(8,128)} %get-tuple-element.20), channel_id=1, source_target_pairs={{0,8},{8,0},{16,248},{24,240},{32,232},{40,224},{48,216},{56,208},... | collective-permute-start | bytes 24584 | tf_op jit(solution)/shard_map/ppermute | solution.py:509
  13.6 7.3 %copy-start.5 = (s32[1,4]{1,0:T(1,128)S(1)}, s32[1,4]{1,0:T(1,128)}, u32[]{:S(2)}) copy-start(s32[1,4]{1,0:T(1,128)} %links.3) | copy-start | bytes 52
  13.6 7.2 %collective-permute-start.4 = (f32[16,128]{1,0:T(8,128)}, f32[16,128]{1,0:T(8,128)S(1)}, u32[]{:S(2)}, u32[]{:S(2)}) collective-permute-start(f32[16,128]{1,0:T(8,128)} %get-tuple-element.21), channel_id=1, source_target_pairs={{0,248},{8,240},{16,232},{24,224},{32,216},{40,208},{48,200},{56,1... | collective-permute-start | bytes 24584 | tf_op jit(solution)/shard_map/ppermute | solution.py:509

commit v4 on v3

--- a/solution.py
+++ b/solution.py
@@ -16,6 +16,7 @@
 TOP = 24
 NORTH = 5
 CHUNKS = 8
+PACK_ROWS = 128
 SLOT = (0, 4, 2, 6, 1, 5, 3, 7)
 TILES = ((0, 1), (2, 3), (4, 5), (6, 7))
 W_SHIFT = (-4, -36, -20, -52)
@@ -72,30 +73,38 @@
     return out + [land, strided(kx, (), t, half, ROWS), strided(ky, (), t, half, ROWS)]
 
 
-def pack_kernel(links, *refs):
-    field, kx, ky, sea = paired(refs[:8])
-    west, east, north, nw, ne, rows = refs[8:]
+def pack_kernel(links, field, kx, ky, sea, west, east, north, nw, ne, rows):
     lane = lanes()
     group = lane // 16
-    for t in range(ROWS):
-        low = planes_at(field, kx, ky, sea, t, 0)
-        high = planes_at(field, kx, ky, sea, t, 1)
+    start = PACK_ROWS * pl.program_id(0)
+
+    def planes(at, cols):
+        land = sea[at, cols].astype(jnp.float32)
+        return [field[l, at, cols] * land for l in range(LEV)] + [land, kx[at, cols], ky[at, cols]]
+
+    for t in range(PACK_ROWS // 8):
+        at = slice(8 * t, 8 * t + 8)
+        low, high = planes(at, slice(0, 128)), planes(at, slice(128, 256))
         w, e = low[0], roll(high[0], 16)
         for p in range(1, PLANES):
             w = jnp.where(group == SLOT[p], roll(low[p], 16 * SLOT[p]), w)
             e = jnp.where(group == SLOT[p], roll(high[p], 16 * SLOT[p] + 16), e)
-        west[8 * t : 8 * t + 8, :] = w
-        east[8 * t : 8 * t + 8, :] = e
+        to = pl.ds(pl.multiple_of(start + 8 * t, 8), 8)
+        west[to, :] = w
+        east[to, :] = e
+
+    @pl.when(pl.program_id(0) == SIDE // PACK_ROWS - 1)
+    def _():
+        pack_top(links, planes, west, east, north, nw, ne, rows)
+
+
+def pack_top(links, planes, west, east, north, nw, ne, rows):
+    lane = lanes()
     flip = 127 - lane
-    for p in range(PLANES):
-        for o in range(2):
-            for half in range(2):
-                at = pl.ds(SIDE - 16 + 8 * o, 8)
-                if p <= LEV:
-                    x = sea[half][at, :].astype(jnp.float32)
-                    x = field[half][p, at, :] * x if p < LEV else x
-                else:
-                    x = (kx, ky)[p - LEV - 1][half][at, :]
+    for o in range(2):
+        for half in range(2):
+            at = slice(PACK_ROWS - 16 + 8 * o, PACK_ROWS - 8 + 8 * o)
+            for p, x in enumerate(planes(at, slice(128 * half, 128 * half + 128))):
                 x = jnp.take_along_axis(x, flip, axis=1)
                 rows[p, 8 * o : 8 * o + 8, 128 * (1 - half) : 128 * (1 - half) + 128] = x
     for k in range(16):
@@ -106,7 +115,7 @@
     north[LEV, 15, :] = jnp.full((SIDE,), 1.0, jnp.float32) * east_open
     swap = jnp.bitwise_xor(lane, 15)
     for k in range(16):
-        r = 8 * (ROWS - 1 - k) + 7
+        r = SIDE - 1 - k
         nw[k : k + 1, :] = west[r : r + 1, :]
         ne[k : k + 1, :] = east[r : r + 1, :]
     for o in range(2):
@@ -120,13 +129,15 @@
     return pl.pallas_call(
         pack_kernel,
         out_shape=[jax.ShapeDtypeStruct(s, f32) for s in shapes],
-        grid=(1,),
-        in_specs=[SMEM] + half_specs((LEV,), (), (), ()),
+        grid=(SIDE // PACK_ROWS,),
+        in_specs=[SMEM]
+        + [pl.BlockSpec((LEV, PACK_ROWS, SIDE), lambda i: (0, i, 0))]
+        + [pl.BlockSpec((PACK_ROWS, SIDE), lambda i: (i, 0))] * 3,
         out_specs=[VMEM] * 5,
         scratch_shapes=[pltpu.VMEM((PLANES, 16, SIDE), f32)],
         compiler_params=pltpu.CompilerParams(vmem_limit_bytes=60 << 20),
         name="pack",
-    )(links, *doubled(field, kx, ky, sea))
+    )(links, field, kx, ky, sea)
 
 
 EVEN, ODD = slice(0, 128), slice(128, 256)
@@ -311,7 +322,7 @@
     def fill(b, none):
         for j in range(8):
             t = 8 * b + j
-            at = pl.ds(pl.multiple_of(8 * t, 8), 8)
+            at = pl.ds(t, 8, stride=ROWS)
             w, e = west[at, :], east[at, :]
             for i in range(4):
                 strips[i][t] = with_halo(i, own[i, t], w, e)

time: 82 us -> 81.1 us (0.989)
  Pallas kernels: 20.1 us -> 19.2 us
    pallas_call x1, Pallas kernels: 3.89 us -> 2.92 us  [pack(): pl.pallas_call(pack_kernel, out_shape=[jax.ShapeDtypeStruct(s, f32) for s...]
where the time goes in v4:
time: 81.1 us; the launch traced here: 80.9 us
  blocking collectives  51.9 us (64%)
  Pallas kernels  19.2 us (24%)
  starting transfers between devices  9.71 us (12%)
    all_to_all x1, blocking collectives, shards(): gathered = lax.all_to_all(smooth, 'lev', 0, 0, tiled=True)  28.8 us
    all_to_all x1, blocking collectives, shards(): back = lax.all_to_all(mix(gathered, mixer), 'lev', 0, 0, tiled=True)  23.1 us
    ppermute x5, starting transfers between devices, send(): lax.ppermute(x, 'tile', [(i, target(i) % tiles) for i in range(tiles)])  9.71 us
    pallas_call x1, Pallas kernels, inner(): pl.pallas_call(inner_kernel, out_shape=[jax.ShapeDtypeStruct(s, f32) for...  7.15 us
    pallas_call x1, Pallas kernels, rim(): pl.pallas_call(rim_kernel, out_shape=jax.ShapeDtypeStruct((CHUNKS, LEV, S...  6.43 us
    pallas_call x1, Pallas kernels, pack(): pl.pallas_call(pack_kernel, out_shape=[jax.ShapeDtypeStruct(s, f32) for s...  2.92 us
    pallas_call x1, Pallas kernels, unpack(): pl.pallas_call(unpack_kernel, out_shape=jax.ShapeDtypeStruct((LEV, SIDE,...  1.99 us
  transfers between devices with their start and end apart: 5, of which 0 were waited for; matrix products, arithmetic and copies ran while one was open for 0% of the time, Pallas kernels for 9%

profile of v4, /device:TPU:15, one launch (start us, length us, event | category | flops | bytes accessed | tf_op | source)
XLA Modules:
  0.0 80.9 jit_solution(10422710210277381741)
XLA Ops:
  0.0 0.0 copy-start.3
  0.0 0.0 copy-start.2
  0.0 0.0 copy-start.1
  0.0 0.0 copy-start
  0.0 0.0 copy-start.4
  0.0 2.9 %pack.1 = (f32[256,128]{1,0:T(8,128)}, f32[256,128]{1,0:T(8,128)}, f32[8,16,256]{2,1,0:T(8,128)}, f32[16,128]{1,0:T(8,128)}, f32[16,128]{1,0:T(8,128)}) custom-call(s32[1,4]{1,0:T(1,128)} %links.3, f32[5,256,256]{2,1,0:T(8,128)} %bitcast.5, f32[256,256]{1,0:T(8,128)} %bitcast.8, f32[256,256]{1,0:T(8,128)} %bitcast.11, s32[256,256]{1,0:T(8,128)} %bitcast.14), custom_call_target="tpu_custom_call" | custom-call | tf_op jit(solution)/shard_map/pack/pallas_call | solution.py:129
  3.0 1.9 %collective-permute-start = (f32[256,128]{1,0:T(8,128)}, f32[256,128]{1,0:T(8,128)S(1)}, u32[]{:S(2)}, u32[]{:S(2)}) collective-permute-start(f32[256,128]{1,0:T(8,128)} %get-tuple-element.17), channel_id=1, source_target_pairs={{0,8},{8,16},{16,24},{24,32},{32,40},{40,48},{48,56},{56,64},{64,7... | collective-permute-start | bytes 393224 | tf_op jit(solution)/shard_map/ppermute | solution.py:520
  4.9 0.0 collective-permute-start.1
  4.9 2.8 %collective-permute-start.2 = (f32[8,16,256]{2,1,0:T(8,128)}, f32[8,16,256]{2,1,0:T(8,128)S(1)}, u32[]{:S(2)}, u32[]{:S(2)}) collective-permute-start(f32[8,16,256]{2,1,0:T(8,128)} %get-tuple-element.19), channel_id=1, source_target_pairs={{0,0},{8,248},{16,240},{24,232},{32,224},{40,216},{48,208},{56,200... | collective-permute-start | bytes 393224 | tf_op jit(solution)/shard_map/ppermute | solution.py:520
  7.7 5.0 %collective-permute-start.3 = (f32[16,128]{1,0:T(8,128)}, f32[16,128]{1,0:T(8,128)S(1)}, u32[]{:S(2)}, u32[]{:S(2)}) collective-permute-start(f32[16,128]{1,0:T(8,128)} %get-tuple-element.20), channel_id=1, source_target_pairs={{0,8},{8,0},{16,248},{24,240},{32,232},{40,224},{48,216},{56,208},... | collective-permute-start | bytes 24584 | tf_op jit(solution)/shard_map/ppermute | solution.py:520
  12.7 0.0 copy-start.5
  12.7 0.0 collective-permute-start.4
  12.7 0.0 copy-done.3
  12.7 0.0 copy-done.2
  12.7 0.0 copy-done.1
  12.7 0.0 copy-done
  12.7 0.0 copy-done.4
  12.7 7.1 %inner.1 = (f32[5,33,8,256]{3,2,1,0:T(8,128)S(1)}, f32[4,32,8,128]{3,2,1,0:T(8,128)S(1)}, f32[8,24,256]{2,1,0:T(8,128)S(1)}, bf16[640,640]{1,0:T(8,128)(2,1)S(1)}) custom-call(f32[5,256,256]{2,1,0:T(8,128)S(1)} %bitcast.6, f32[5,256,256]{2,1,0:T(8,128)S(1)} %bitcast.7, f32[256,256]{1,0:T(8,128)S(1)} %bitcast.9, f32[256,256]{1,0:T(8,128)S(1)} %bitcast.10, ...), custom_call_target="tpu_custom_call" | custom-call | flops 40000000 | bytes 40000000 | tf_op jit(solution)/shard_map/inner/pallas_call | solution.py:280
  19.9 0.0 collective-permute-done.3.nw
  19.9 0.0 collective-permute-done.4.ne
  19.9 0.0 collective-permute-done.west
  19.9 0.0 collective-permute-done.1.east
  19.9 0.0 collective-permute-done.2.north
  19.9 0.0 copy-done.5
  19.9 6.4 %rim.1 = bf16[8,5,32,256]{3,2,1,0:T(8,128)(2,1)S(1)} custom-call(s32[1,4]{1,0:T(1,128)S(1)} %copy-done.5, f32[5,33,8,256]{3,2,1,0:T(8,128)S(1)} %get-tuple-element.14.inside, f32[4,32,8,128]{3,2,1,0:T(8,128)S(1)} %get-tuple-element.15.own, f32[8,24,256]{2,1,0:T(8,128)S(1)} %get-tuple-element.16.top, f32[256,128]{1,0:T(8,128)S(1)} %collective-permute-done.west, ...), custom_call_target="tpu_custom_call" | custom-call | tf_op jit(solution)/shard_map/rim/pallas_call | solution.py:463
  26.4 28.8 %all_to_all.10.x = bf16[8,5,32,256]{3,2,1,0:T(8,128)(2,1)S(1)} all-to-all(bf16[8,5,32,256]{3,2,1,0:T(8,128)(2,1)S(1)} %rim.1), channel_id=1, replica_groups=mesh['tile'=32,'lev'=8] {'lev'}, dimensions={0} | all-to-all | bytes 1310720 | tf_op jit(solution)/shard_map/all_to_all | solution.py:531
  55.1 0.7 mix.1
  55.8 23.1 %all_to_all.11.z = bf16[8,5,32,256]{3,2,1,0:T(8,128)(2,1)S(1)} all-to-all(bf16[8,5,32,256]{3,2,1,0:T(8,128)(2,1)S(1)} %mix.1), channel_id=1, replica_groups=mesh['tile'=32,'lev'=8] {'lev'}, dimensions={0} | all-to-all | bytes 1310720 | tf_op jit(solution)/shard_map/all_to_all | solution.py:532
  78.9 2.0 %unpack.1 = f32[5,256,256]{2,1,0:T(8,128)} custom-call(bf16[8,5,32,256]{3,2,1,0:T(8,128)(2,1)S(1)} %all_to_all.11.z), custom_call_target="tpu_custom_call" | custom-call | tf_op jit(solution)/shard_map/unpack/pallas_call | solution.py:505
Async XLA Ops:
  0.0 12.7 %copy-start.3 = (s32[1,256,256]{2,1,0:T(8,128)S(1)}, s32[1,256,256]{2,1,0:T(8,128)}, u32[]{:S(2)}) copy-start(s32[1,256,256]{2,1,0:T(8,128)} %param.9) | copy-start | bytes 786436
  0.0 12.7 %copy-start.2 = (f32[1,256,256]{2,1,0:T(8,128)S(1)}, f32[1,256,256]{2,1,0:T(8,128)}, u32[]{:S(2)}) copy-start(f32[1,256,256]{2,1,0:T(8,128)} %param.8) | copy-start | bytes 786436
  0.0 12.7 %copy-start.1 = (f32[1,256,256]{2,1,0:T(8,128)S(1)}, f32[1,256,256]{2,1,0:T(8,128)}, u32[]{:S(2)}) copy-start(f32[1,256,256]{2,1,0:T(8,128)} %param.7) | copy-start | bytes 786436
  0.0 12.7 %copy-start = (f32[1,5,256,256]{3,2,1,0:T(8,128)S(1)}, f32[1,5,256,256]{3,2,1,0:T(8,128)}, u32[]{:S(2)}) copy-start(f32[1,5,256,256]{3,2,1,0:T(8,128)} %param.6) | copy-start | bytes 3932164
  0.0 12.7 %copy-start.4 = (bf16[40,40]{1,0:T(8,128)(2,1)S(1)}, bf16[40,40]{1,0:T(8,128)(2,1)}, u32[]{:S(2)}) copy-start(bf16[40,40]{1,0:T(8,128)(2,1)} %refs_8_.1) | copy-start | bytes 9604
  3.0 16.9 %collective-permute-start = (f32[256,128]{1,0:T(8,128)}, f32[256,128]{1,0:T(8,128)S(1)}, u32[]{:S(2)}, u32[]{:S(2)}) collective-permute-start(f32[256,128]{1,0:T(8,128)} %get-tuple-element.17), channel_id=1, source_target_pairs={{0,8},{8,16},{16,24},{24,32},{32,40},{40,48},{48,56},{56,64},{64,7... | collective-permute-start | bytes 393224 | tf_op jit(solution)/shard_map/ppermute | solution.py:520
  4.9 15.0 %collective-permute-start.1 = (f32[256,128]{1,0:T(8,128)}, f32[256,128]{1,0:T(8,128)S(1)}, u32[]{:S(2)}, u32[]{:S(2)}) collective-permute-start(f32[256,128]{1,0:T(8,128)} %get-tuple-element.18), channel_id=1, source_target_pairs={{0,248},{8,0},{16,8},{24,16},{32,24},{40,32},{48,40},{56,48},{64,5... | collective-permute-start | bytes 393224 | tf_op jit(solution)/shard_map/ppermute | solution.py:520
  4.9 15.0 %collective-permute-start.2 = (f32[8,16,256]{2,1,0:T(8,128)}, f32[8,16,256]{2,1,0:T(8,128)S(1)}, u32[]{:S(2)}, u32[]{:S(2)}) collective-permute-start(f32[8,16,256]{2,1,0:T(8,128)} %get-tuple-element.19), channel_id=1, source_target_pairs={{0,0},{8,248},{16,240},{24,232},{32,224},{40,216},{48,208},{56,200... | collective-permute-start | bytes 393224 | tf_op jit(solution)/shard_map/ppermute | solution.py:520
  7.7 12.2 %collective-permute-start.3 = (f32[16,128]{1,0:T(8,128)}, f32[16,128]{1,0:T(8,128)S(1)}, u32[]{:S(2)}, u32[]{:S(2)}) collective-permute-start(f32[16,128]{1,0:T(8,128)} %get-tuple-element.20), channel_id=1, source_target_pairs={{0,8},{8,0},{16,248},{24,240},{32,232},{40,224},{48,216},{56,208},... | collective-permute-start | bytes 24584 | tf_op jit(solution)/shard_map/ppermute | solution.py:520
  12.7 7.3 %copy-start.5 = (s32[1,4]{1,0:T(1,128)S(1)}, s32[1,4]{1,0:T(1,128)}, u32[]{:S(2)}) copy-start(s32[1,4]{1,0:T(1,128)} %links.3) | copy-start | bytes 52
  12.7 7.2 %collective-permute-start.4 = (f32[16,128]{1,0:T(8,128)}, f32[16,128]{1,0:T(8,128)S(1)}, u32[]{:S(2)}, u32[]{:S(2)}) collective-permute-start(f32[16,128]{1,0:T(8,128)} %get-tuple-element.21), channel_id=1, source_target_pairs={{0,248},{8,240},{16,232},{24,224},{32,216},{40,208},{48,200},{56,1... | collective-permute-start | bytes 24584 | tf_op jit(solution)/shard_map/ppermute | solution.py:520

commit v5 on v4

--- a/solution.py
+++ b/solution.py
@@ -209,8 +209,12 @@
     def at(shape, axis):
         return lax.broadcasted_iota(jnp.int32, shape, axis)
 
-    left = (at((size, levels), 0) // 16 == at((size, levels), 1)).astype(jnp.float32).astype(jnp.bfloat16)
-    right = (at((levels, size), 1) // 16 == at((levels, size), 0)).astype(jnp.float32).astype(jnp.bfloat16)
+
+    def level(row):
+        return LEV * (CHUNKS - 1 - row // (16 * LEV)) + row // 16 % LEV
+
+    left = (level(at((size, levels), 0)) == at((size, levels), 1)).astype(jnp.float32).astype(jnp.bfloat16)
+    right = (level(at((levels, size), 1)) == at((levels, size), 0)).astype(jnp.float32).astype(jnp.bfloat16)
     tall = jnp.dot(left, vertical, preferred_element_type=jnp.float32).astype(jnp.bfloat16)
     full = jnp.dot(tall, right, preferred_element_type=jnp.float32)
     same = at((size, size), 0) % 16 == at((size, size), 1) % 16
@@ -528,9 +532,11 @@
     from_ne = send(ne, lambda i: -1 - i)
     inside, own, top, mixer = inner(cells, kx, ky, sea, vertical)
     smooth = rim(tile_links, inside, own, top, from_west, from_east, from_north, from_nw, from_ne)
-    gathered = lax.all_to_all(smooth, "lev", 0, 0, tiled=True)
-    back = lax.all_to_all(mix(gathered, mixer), "lev", 0, 0, tiled=True)
-    return unpack(back)[None]
+
+    def turn(x):
+        return lax.all_to_all(x, "lev", 0, 0, axis_index_groups=[list(range(CHUNKS))[::-1]], tiled=True)
+
+    return unpack(turn(mix(turn(smooth), mixer)))[None]
 
 
 def solution(mesh):

time: 81.1 us -> 77.9 us (0.961); the launches traced: 80.9 us -> 76.6 us
  blocking collectives: 51.9 us -> 47.5 us
    all_to_all x2, blocking collectives: 51.9 us -> 47.5 us  [turn(): lax.all_to_all(x, 'lev', 0, 0, axis_index_groups=[list(range(CHUNKS))[::-...]
where the time goes in v5:
time: 77.9 us; the launch traced here: 76.6 us
  blocking collectives  47.5 us (61%)
  Pallas kernels  19.3 us (25%)
  starting transfers between devices  9.71 us (12%)
    all_to_all x2, blocking collectives, turn(): lax.all_to_all(x, 'lev', 0, 0, axis_index_groups=[list(range(CHUNKS))[::-...  47.5 us
    ppermute x5, starting transfers between devices, send(): lax.ppermute(x, 'tile', [(i, target(i) % tiles) for i in range(tiles)])  9.71 us
    pallas_call x1, Pallas kernels, inner(): pl.pallas_call(inner_kernel, out_shape=[jax.ShapeDtypeStruct(s, f32) for...  7.25 us
    pallas_call x1, Pallas kernels, rim(): pl.pallas_call(rim_kernel, out_shape=jax.ShapeDtypeStruct((CHUNKS, LEV, S...  6.43 us
    pallas_call x1, Pallas kernels, pack(): pl.pallas_call(pack_kernel, out_shape=[jax.ShapeDtypeStruct(s, f32) for s...  2.92 us
    pallas_call x1, Pallas kernels, unpack(): pl.pallas_call(unpack_kernel, out_shape=jax.ShapeDtypeStruct((LEV, SIDE,...  1.99 us
  transfers between devices with their start and end apart: 5, of which 0 were waited for; matrix products, arithmetic and copies ran while one was open for 0% of the time, Pallas kernels for 9%

profile of v5, /device:TPU:15, one launch (start us, length us, event | category | flops | bytes accessed | tf_op | source)
XLA Modules:
  0.0 76.6 jit_solution(2271957736869402148)
XLA Ops:
  0.0 0.0 copy-start.3
  0.0 0.0 copy-start.2
  0.0 0.0 copy-start.1
  0.0 0.0 copy-start
  0.0 0.0 copy-start.4
  0.0 2.9 %pack.1 = (f32[256,128]{1,0:T(8,128)}, f32[256,128]{1,0:T(8,128)}, f32[8,16,256]{2,1,0:T(8,128)}, f32[16,128]{1,0:T(8,128)}, f32[16,128]{1,0:T(8,128)}) custom-call(s32[1,4]{1,0:T(1,128)} %links.3, f32[5,256,256]{2,1,0:T(8,128)} %bitcast.5, f32[256,256]{1,0:T(8,128)} %bitcast.8, f32[256,256]{1,0:T(8,128)} %bitcast.11, s32[256,256]{1,0:T(8,128)} %bitcast.14), custom_call_target="tpu_custom_call" | custom-call | tf_op jit(solution)/shard_map/pack/pallas_call | solution.py:129
  3.0 1.9 %collective-permute-start = (f32[256,128]{1,0:T(8,128)}, f32[256,128]{1,0:T(8,128)S(1)}, u32[]{:S(2)}, u32[]{:S(2)}) collective-permute-start(f32[256,128]{1,0:T(8,128)} %get-tuple-element.17), channel_id=1, source_target_pairs={{0,8},{8,16},{16,24},{24,32},{32,40},{40,48},{48,56},{56,64},{64,7... | collective-permute-start | bytes 393224 | tf_op jit(solution)/shard_map/ppermute | solution.py:524
  4.9 0.0 collective-permute-start.1
  4.9 2.8 %collective-permute-start.2 = (f32[8,16,256]{2,1,0:T(8,128)}, f32[8,16,256]{2,1,0:T(8,128)S(1)}, u32[]{:S(2)}, u32[]{:S(2)}) collective-permute-start(f32[8,16,256]{2,1,0:T(8,128)} %get-tuple-element.19), channel_id=1, source_target_pairs={{0,0},{8,248},{16,240},{24,232},{32,224},{40,216},{48,208},{56,200... | collective-permute-start | bytes 393224 | tf_op jit(solution)/shard_map/ppermute | solution.py:524
  7.7 5.0 %collective-permute-start.3 = (f32[16,128]{1,0:T(8,128)}, f32[16,128]{1,0:T(8,128)S(1)}, u32[]{:S(2)}, u32[]{:S(2)}) collective-permute-start(f32[16,128]{1,0:T(8,128)} %get-tuple-element.20), channel_id=1, source_target_pairs={{0,8},{8,0},{16,248},{24,240},{32,232},{40,224},{48,216},{56,208},... | collective-permute-start | bytes 24584 | tf_op jit(solution)/shard_map/ppermute | solution.py:524
  12.7 0.0 copy-start.5
  12.7 0.0 collective-permute-start.4
  12.7 0.0 copy-done.3
  12.7 0.0 copy-done.2
  12.7 0.0 copy-done.1
  12.7 0.0 copy-done
  12.7 0.0 copy-done.4
  12.7 7.2 %inner.1 = (f32[5,33,8,256]{3,2,1,0:T(8,128)S(1)}, f32[4,32,8,128]{3,2,1,0:T(8,128)S(1)}, f32[8,24,256]{2,1,0:T(8,128)S(1)}, bf16[640,640]{1,0:T(8,128)(2,1)S(1)}) custom-call(f32[5,256,256]{2,1,0:T(8,128)S(1)} %bitcast.6, f32[5,256,256]{2,1,0:T(8,128)S(1)} %bitcast.7, f32[256,256]{1,0:T(8,128)S(1)} %bitcast.9, f32[256,256]{1,0:T(8,128)S(1)} %bitcast.10, ...), custom_call_target="tpu_custom_call" | custom-call | flops 40000000 | bytes 40000000 | tf_op jit(solution)/shard_map/inner/pallas_call | solution.py:284
  20.0 0.0 collective-permute-done.3.nw
  20.0 0.0 collective-permute-done.4.ne
  20.0 0.0 collective-permute-done.west
  20.0 0.0 collective-permute-done.1.east
  20.0 0.0 collective-permute-done.2.north
  20.0 0.0 copy-done.5
  20.0 6.4 %rim.1 = bf16[8,5,32,256]{3,2,1,0:T(8,128)(2,1)S(1)} custom-call(s32[1,4]{1,0:T(1,128)S(1)} %copy-done.5, f32[5,33,8,256]{3,2,1,0:T(8,128)S(1)} %get-tuple-element.14.inside, f32[4,32,8,128]{3,2,1,0:T(8,128)S(1)} %get-tuple-element.15.own, f32[8,24,256]{2,1,0:T(8,128)S(1)} %get-tuple-element.16.top, f32[256,128]{1,0:T(8,128)S(1)} %collective-permute-done.west, ...), custom_call_target="tpu_custom_call" | custom-call | tf_op jit(solution)/shard_map/rim/pallas_call | solution.py:467
  26.5 24.1 %all_to_all.10.x = bf16[8,5,32,256]{3,2,1,0:T(8,128)(2,1)S(1)} all-to-all(bf16[8,5,32,256]{3,2,1,0:T(8,128)(2,1)S(1)} %rim.1), channel_id=1, replica_groups={{7,6,5,4,3,2,1,0},{15,14,13,12,11,10,9,8},{23,22,21,20,19,18,17,16},{31..., dimensions={0} | all-to-all | bytes 1310720 | tf_op jit(solution)/shard_map/all_to_all | solution.py:537
  50.6 0.7 mix.1
  51.3 23.3 %all_to_all.11.z = bf16[8,5,32,256]{3,2,1,0:T(8,128)(2,1)S(1)} all-to-all(bf16[8,5,32,256]{3,2,1,0:T(8,128)(2,1)S(1)} %mix.1), channel_id=1, replica_groups={{7,6,5,4,3,2,1,0},{15,14,13,12,11,10,9,8},{23,22,21,20,19,18,17,16},{31..., dimensions={0} | all-to-all | bytes 1310720 | tf_op jit(solution)/shard_map/all_to_all | solution.py:537
  74.6 2.0 %unpack.1 = f32[5,256,256]{2,1,0:T(8,128)} custom-call(bf16[8,5,32,256]{3,2,1,0:T(8,128)(2,1)S(1)} %all_to_all.11.z), custom_call_target="tpu_custom_call" | custom-call | tf_op jit(solution)/shard_map/unpack/pallas_call | solution.py:509
Async XLA Ops:
  0.0 12.7 %copy-start.3 = (s32[1,256,256]{2,1,0:T(8,128)S(1)}, s32[1,256,256]{2,1,0:T(8,128)}, u32[]{:S(2)}) copy-start(s32[1,256,256]{2,1,0:T(8,128)} %param.9) | copy-start | bytes 786436
  0.0 12.7 %copy-start.2 = (f32[1,256,256]{2,1,0:T(8,128)S(1)}, f32[1,256,256]{2,1,0:T(8,128)}, u32[]{:S(2)}) copy-start(f32[1,256,256]{2,1,0:T(8,128)} %param.8) | copy-start | bytes 786436
  0.0 12.7 %copy-start.1 = (f32[1,256,256]{2,1,0:T(8,128)S(1)}, f32[1,256,256]{2,1,0:T(8,128)}, u32[]{:S(2)}) copy-start(f32[1,256,256]{2,1,0:T(8,128)} %param.7) | copy-start | bytes 786436
  0.0 12.7 %copy-start = (f32[1,5,256,256]{3,2,1,0:T(8,128)S(1)}, f32[1,5,256,256]{3,2,1,0:T(8,128)}, u32[]{:S(2)}) copy-start(f32[1,5,256,256]{3,2,1,0:T(8,128)} %param.6) | copy-start | bytes 3932164
  0.0 12.7 %copy-start.4 = (bf16[40,40]{1,0:T(8,128)(2,1)S(1)}, bf16[40,40]{1,0:T(8,128)(2,1)}, u32[]{:S(2)}) copy-start(bf16[40,40]{1,0:T(8,128)(2,1)} %refs_8_.1) | copy-start | bytes 9604
  3.0 17.0 %collective-permute-start = (f32[256,128]{1,0:T(8,128)}, f32[256,128]{1,0:T(8,128)S(1)}, u32[]{:S(2)}, u32[]{:S(2)}) collective-permute-start(f32[256,128]{1,0:T(8,128)} %get-tuple-element.17), channel_id=1, source_target_pairs={{0,8},{8,16},{16,24},{24,32},{32,40},{40,48},{48,56},{56,64},{64,7... | collective-permute-start | bytes 393224 | tf_op jit(solution)/shard_map/ppermute | solution.py:524
  4.9 15.1 %collective-permute-start.1 = (f32[256,128]{1,0:T(8,128)}, f32[256,128]{1,0:T(8,128)S(1)}, u32[]{:S(2)}, u32[]{:S(2)}) collective-permute-start(f32[256,128]{1,0:T(8,128)} %get-tuple-element.18), channel_id=1, source_target_pairs={{0,248},{8,0},{16,8},{24,16},{32,24},{40,32},{48,40},{56,48},{64,5... | collective-permute-start | bytes 393224 | tf_op jit(solution)/shard_map/ppermute | solution.py:524
  4.9 15.1 %collective-permute-start.2 = (f32[8,16,256]{2,1,0:T(8,128)}, f32[8,16,256]{2,1,0:T(8,128)S(1)}, u32[]{:S(2)}, u32[]{:S(2)}) collective-permute-start(f32[8,16,256]{2,1,0:T(8,128)} %get-tuple-element.19), channel_id=1, source_target_pairs={{0,0},{8,248},{16,240},{24,232},{32,224},{40,216},{48,208},{56,200... | collective-permute-start | bytes 393224 | tf_op jit(solution)/shard_map/ppermute | solution.py:524
  7.7 12.3 %collective-permute-start.3 = (f32[16,128]{1,0:T(8,128)}, f32[16,128]{1,0:T(8,128)S(1)}, u32[]{:S(2)}, u32[]{:S(2)}) collective-permute-start(f32[16,128]{1,0:T(8,128)} %get-tuple-element.20), channel_id=1, source_target_pairs={{0,8},{8,0},{16,248},{24,240},{32,232},{40,224},{48,216},{56,208},... | collective-permute-start | bytes 24584 | tf_op jit(solution)/shard_map/ppermute | solution.py:524
  12.7 7.4 %copy-start.5 = (s32[1,4]{1,0:T(1,128)S(1)}, s32[1,4]{1,0:T(1,128)}, u32[]{:S(2)}) copy-start(s32[1,4]{1,0:T(1,128)} %links.3) | copy-start | bytes 52
  12.7 7.3 %collective-permute-start.4 = (f32[16,128]{1,0:T(8,128)}, f32[16,128]{1,0:T(8,128)S(1)}, u32[]{:S(2)}, u32[]{:S(2)}) collective-permute-start(f32[16,128]{1,0:T(8,128)} %get-tuple-element.21), channel_id=1, source_target_pairs={{0,248},{8,240},{16,232},{24,224},{32,216},{40,208},{48,200},{56,1... | collective-permute-start | bytes 24584 | tf_op jit(solution)/shard_map/ppermute | solution.py:524

commit v6 on v5

--- a/solution.py
+++ b/solution.py
@@ -510,7 +510,7 @@
         unpack_kernel,
         out_shape=jax.ShapeDtypeStruct((LEV, SIDE, SIDE), jnp.float32),
         grid=(2,),
-        in_specs=[pl.BlockSpec((CHUNKS, LEV, SIDE // CHUNKS, SIDE), lambda h: (0, 0, 0, 0))],
+        in_specs=[VMEM],
         out_specs=pl.BlockSpec((LEV, SIDE, 128), lambda h: (0, 0, h)),
         compiler_params=pltpu.CompilerParams(vmem_limit_bytes=24 << 20),
         name="unpack",

time: 77.9 us -> 77.9 us (level)
  no operation moved by 1% of the time
where the time goes in v6:
time: 77.9 us; the launch traced here: 76.6 us
  blocking collectives  47.5 us (61%)
  Pallas kernels  19.3 us (25%)
  starting transfers between devices  9.71 us (12%)
    all_to_all x2, blocking collectives, turn(): lax.all_to_all(x, 'lev', 0, 0, axis_index_groups=[list(range(CHUNKS))[::-...  47.5 us
    ppermute x5, starting transfers between devices, send(): lax.ppermute(x, 'tile', [(i, target(i) % tiles) for i in range(tiles)])  9.71 us
    pallas_call x1, Pallas kernels, inner(): pl.pallas_call(inner_kernel, out_shape=[jax.ShapeDtypeStruct(s, f32) for...  7.25 us
    pallas_call x1, Pallas kernels, rim(): pl.pallas_call(rim_kernel, out_shape=jax.ShapeDtypeStruct((CHUNKS, LEV, S...  6.43 us
    pallas_call x1, Pallas kernels, pack(): pl.pallas_call(pack_kernel, out_shape=[jax.ShapeDtypeStruct(s, f32) for s...  2.92 us
    pallas_call x1, Pallas kernels, unpack(): pl.pallas_call(unpack_kernel, out_shape=jax.ShapeDtypeStruct((LEV, SIDE,...  1.99 us
  transfers between devices with their start and end apart: 5, of which 0 were waited for; matrix products, arithmetic and copies ran while one was open for 0% of the time, Pallas kernels for 9%

profile of v6, /device:TPU:15, one launch (start us, length us, event | category | flops | bytes accessed | tf_op | source)
XLA Modules:
  0.0 76.6 jit_solution(2271957736869402148)
XLA Ops:
  0.0 0.0 copy-start.3
  0.0 0.0 copy-start.2
  0.0 0.0 copy-start.1
  0.0 0.0 copy-start
  0.0 0.0 copy-start.4
  0.0 2.9 %pack.1 = (f32[256,128]{1,0:T(8,128)}, f32[256,128]{1,0:T(8,128)}, f32[8,16,256]{2,1,0:T(8,128)}, f32[16,128]{1,0:T(8,128)}, f32[16,128]{1,0:T(8,128)}) custom-call(s32[1,4]{1,0:T(1,128)} %links.3, f32[5,256,256]{2,1,0:T(8,128)} %bitcast.5, f32[256,256]{1,0:T(8,128)} %bitcast.8, f32[256,256]{1,0:T(8,128)} %bitcast.11, s32[256,256]{1,0:T(8,128)} %bitcast.14), custom_call_target="tpu_custom_call" | custom-call | tf_op jit(solution)/shard_map/pack/pallas_call | solution.py:129
  3.0 1.9 %collective-permute-start = (f32[256,128]{1,0:T(8,128)}, f32[256,128]{1,0:T(8,128)S(1)}, u32[]{:S(2)}, u32[]{:S(2)}) collective-permute-start(f32[256,128]{1,0:T(8,128)} %get-tuple-element.17), channel_id=1, source_target_pairs={{0,8},{8,16},{16,24},{24,32},{32,40},{40,48},{48,56},{56,64},{64,7... | collective-permute-start | bytes 393224 | tf_op jit(solution)/shard_map/ppermute | solution.py:524
  4.9 0.0 collective-permute-start.1
  4.9 2.8 %collective-permute-start.2 = (f32[8,16,256]{2,1,0:T(8,128)}, f32[8,16,256]{2,1,0:T(8,128)S(1)}, u32[]{:S(2)}, u32[]{:S(2)}) collective-permute-start(f32[8,16,256]{2,1,0:T(8,128)} %get-tuple-element.19), channel_id=1, source_target_pairs={{0,0},{8,248},{16,240},{24,232},{32,224},{40,216},{48,208},{56,200... | collective-permute-start | bytes 393224 | tf_op jit(solution)/shard_map/ppermute | solution.py:524
  7.7 5.0 %collective-permute-start.3 = (f32[16,128]{1,0:T(8,128)}, f32[16,128]{1,0:T(8,128)S(1)}, u32[]{:S(2)}, u32[]{:S(2)}) collective-permute-start(f32[16,128]{1,0:T(8,128)} %get-tuple-element.20), channel_id=1, source_target_pairs={{0,8},{8,0},{16,248},{24,240},{32,232},{40,224},{48,216},{56,208},... | collective-permute-start | bytes 24584 | tf_op jit(solution)/shard_map/ppermute | solution.py:524
  12.7 0.0 copy-start.5
  12.7 0.0 collective-permute-start.4
  12.7 0.0 copy-done.3
  12.7 0.0 copy-done.2
  12.7 0.0 copy-done.1
  12.7 0.0 copy-done
  12.7 0.0 copy-done.4
  12.7 7.2 %inner.1 = (f32[5,33,8,256]{3,2,1,0:T(8,128)S(1)}, f32[4,32,8,128]{3,2,1,0:T(8,128)S(1)}, f32[8,24,256]{2,1,0:T(8,128)S(1)}, bf16[640,640]{1,0:T(8,128)(2,1)S(1)}) custom-call(f32[5,256,256]{2,1,0:T(8,128)S(1)} %bitcast.6, f32[5,256,256]{2,1,0:T(8,128)S(1)} %bitcast.7, f32[256,256]{1,0:T(8,128)S(1)} %bitcast.9, f32[256,256]{1,0:T(8,128)S(1)} %bitcast.10, ...), custom_call_target="tpu_custom_call" | custom-call | flops 40000000 | bytes 40000000 | tf_op jit(solution)/shard_map/inner/pallas_call | solution.py:284
  20.0 0.0 collective-permute-done.3.nw
  20.0 0.0 collective-permute-done.4.ne
  20.0 0.0 collective-permute-done.west
  20.0 0.0 collective-permute-done.1.east
  20.0 0.0 collective-permute-done.2.north
  20.0 0.0 copy-done.5
  20.0 6.4 %rim.1 = bf16[8,5,32,256]{3,2,1,0:T(8,128)(2,1)S(1)} custom-call(s32[1,4]{1,0:T(1,128)S(1)} %copy-done.5, f32[5,33,8,256]{3,2,1,0:T(8,128)S(1)} %get-tuple-element.14.inside, f32[4,32,8,128]{3,2,1,0:T(8,128)S(1)} %get-tuple-element.15.own, f32[8,24,256]{2,1,0:T(8,128)S(1)} %get-tuple-element.16.top, f32[256,128]{1,0:T(8,128)S(1)} %collective-permute-done.west, ...), custom_call_target="tpu_custom_call" | custom-call | tf_op jit(solution)/shard_map/rim/pallas_call | solution.py:467
  26.5 24.1 %all_to_all.10.x = bf16[8,5,32,256]{3,2,1,0:T(8,128)(2,1)S(1)} all-to-all(bf16[8,5,32,256]{3,2,1,0:T(8,128)(2,1)S(1)} %rim.1), channel_id=1, replica_groups={{7,6,5,4,3,2,1,0},{15,14,13,12,11,10,9,8},{23,22,21,20,19,18,17,16},{31..., dimensions={0} | all-to-all | bytes 1310720 | tf_op jit(solution)/shard_map/all_to_all | solution.py:537
  50.6 0.7 mix.1
  51.3 23.3 %all_to_all.11.z = bf16[8,5,32,256]{3,2,1,0:T(8,128)(2,1)S(1)} all-to-all(bf16[8,5,32,256]{3,2,1,0:T(8,128)(2,1)S(1)} %mix.1), channel_id=1, replica_groups={{7,6,5,4,3,2,1,0},{15,14,13,12,11,10,9,8},{23,22,21,20,19,18,17,16},{31..., dimensions={0} | all-to-all | bytes 1310720 | tf_op jit(solution)/shard_map/all_to_all | solution.py:537
  74.6 2.0 %unpack.1 = f32[5,256,256]{2,1,0:T(8,128)} custom-call(bf16[8,5,32,256]{3,2,1,0:T(8,128)(2,1)S(1)} %all_to_all.11.z), custom_call_target="tpu_custom_call" | custom-call | tf_op jit(solution)/shard_map/unpack/pallas_call | solution.py:509
Async XLA Ops:
  0.0 12.7 %copy-start.3 = (s32[1,256,256]{2,1,0:T(8,128)S(1)}, s32[1,256,256]{2,1,0:T(8,128)}, u32[]{:S(2)}) copy-start(s32[1,256,256]{2,1,0:T(8,128)} %param.9) | copy-start | bytes 786436
  0.0 12.7 %copy-start.2 = (f32[1,256,256]{2,1,0:T(8,128)S(1)}, f32[1,256,256]{2,1,0:T(8,128)}, u32[]{:S(2)}) copy-start(f32[1,256,256]{2,1,0:T(8,128)} %param.8) | copy-start | bytes 786436
  0.0 12.7 %copy-start.1 = (f32[1,256,256]{2,1,0:T(8,128)S(1)}, f32[1,256,256]{2,1,0:T(8,128)}, u32[]{:S(2)}) copy-start(f32[1,256,256]{2,1,0:T(8,128)} %param.7) | copy-start | bytes 786436
  0.0 12.7 %copy-start = (f32[1,5,256,256]{3,2,1,0:T(8,128)S(1)}, f32[1,5,256,256]{3,2,1,0:T(8,128)}, u32[]{:S(2)}) copy-start(f32[1,5,256,256]{3,2,1,0:T(8,128)} %param.6) | copy-start | bytes 3932164
  0.0 12.7 %copy-start.4 = (bf16[40,40]{1,0:T(8,128)(2,1)S(1)}, bf16[40,40]{1,0:T(8,128)(2,1)}, u32[]{:S(2)}) copy-start(bf16[40,40]{1,0:T(8,128)(2,1)} %refs_8_.1) | copy-start | bytes 9604
  3.0 17.0 %collective-permute-start = (f32[256,128]{1,0:T(8,128)}, f32[256,128]{1,0:T(8,128)S(1)}, u32[]{:S(2)}, u32[]{:S(2)}) collective-permute-start(f32[256,128]{1,0:T(8,128)} %get-tuple-element.17), channel_id=1, source_target_pairs={{0,8},{8,16},{16,24},{24,32},{32,40},{40,48},{48,56},{56,64},{64,7... | collective-permute-start | bytes 393224 | tf_op jit(solution)/shard_map/ppermute | solution.py:524
  4.9 15.1 %collective-permute-start.1 = (f32[256,128]{1,0:T(8,128)}, f32[256,128]{1,0:T(8,128)S(1)}, u32[]{:S(2)}, u32[]{:S(2)}) collective-permute-start(f32[256,128]{1,0:T(8,128)} %get-tuple-element.18), channel_id=1, source_target_pairs={{0,248},{8,0},{16,8},{24,16},{32,24},{40,32},{48,40},{56,48},{64,5... | collective-permute-start | bytes 393224 | tf_op jit(solution)/shard_map/ppermute | solution.py:524
  4.9 15.1 %collective-permute-start.2 = (f32[8,16,256]{2,1,0:T(8,128)}, f32[8,16,256]{2,1,0:T(8,128)S(1)}, u32[]{:S(2)}, u32[]{:S(2)}) collective-permute-start(f32[8,16,256]{2,1,0:T(8,128)} %get-tuple-element.19), channel_id=1, source_target_pairs={{0,0},{8,248},{16,240},{24,232},{32,224},{40,216},{48,208},{56,200... | collective-permute-start | bytes 393224 | tf_op jit(solution)/shard_map/ppermute | solution.py:524
  7.7 12.3 %collective-permute-start.3 = (f32[16,128]{1,0:T(8,128)}, f32[16,128]{1,0:T(8,128)S(1)}, u32[]{:S(2)}, u32[]{:S(2)}) collective-permute-start(f32[16,128]{1,0:T(8,128)} %get-tuple-element.20), channel_id=1, source_target_pairs={{0,8},{8,0},{16,248},{24,240},{32,232},{40,224},{48,216},{56,208},... | collective-permute-start | bytes 24584 | tf_op jit(solution)/shard_map/ppermute | solution.py:524
  12.7 7.4 %copy-start.5 = (s32[1,4]{1,0:T(1,128)S(1)}, s32[1,4]{1,0:T(1,128)}, u32[]{:S(2)}) copy-start(s32[1,4]{1,0:T(1,128)} %links.3) | copy-start | bytes 52
  12.7 7.3 %collective-permute-start.4 = (f32[16,128]{1,0:T(8,128)}, f32[16,128]{1,0:T(8,128)S(1)}, u32[]{:S(2)}, u32[]{:S(2)}) collective-permute-start(f32[16,128]{1,0:T(8,128)} %get-tuple-element.21), channel_id=1, source_target_pairs={{0,248},{8,240},{16,232},{24,224},{32,216},{40,208},{48,200},{56,1... | collective-permute-start | bytes 24584 | tf_op jit(solution)/shard_map/ppermute | solution.py:524
